TPU v7x, 256 devices: a whole 4x4x8 slice. The times are simulated.
256 devices in a mesh: lon: 64 (over z, x_hi, y), lat: 4 (over x_lo, core).
Axes of the slice: x: 4 (x_hi: 2, x_lo: 2; x = x_hi * 2 + x_lo), y: 4, z: 8, core: 2. Of those that a mesh axis runs over, the one named last changes fastest.
Arguments:
- control: float32 [4, 128, 1024, 128], P(None, 'lat', 'lon'), may hold values from -6 to 6
- observed: float32 [4, 128, 1024, 128], P(None, 'lat', 'lon'), may hold values from -6 to 6
- deviation: float32 [4, 128, 1024, 128], P(None, 'lat', 'lon'), may hold values from 0.3 to 3
- obs_weight: float32 [128, 1024], P('lat', 'lon'), may hold values from 0.5 to 2
- diffusivity: float32 [128, 1024], P('lat', 'lon'), may hold values from 0.05 to 0.24
- region_map: int32 [128, 1024], P('lat', 'lon'), may hold values from 0 to 15, as said below
- correlation: float32 [16, 4, 128, 128], replicated, as said below
Outputs:
- gradient: float32 [4, 128, 1024, 128], P(None, 'lat', 'lon')
Inputs may be any that keep to these rules, and one draw needn't show every extreme that they name: `region_map`: constant on aligned tiles of 4 latitudes by 8 longitudes; every region appears somewhere. `correlation`: each matrix is a diagonal with entries from 0.8 to 1.2 plus independent entries of deviation about 0.6 / sqrt(128).
All inputs are finite; a program needn't handle non-finite values.
Results may differ from a plain program's by a relative error of at most 0.000057.
Values sent between devices are 32-bit elements; how exact they have to be, the bound alone decides.
A program may use at most 64 MiB of HBM per device.

v0:
```python
import jax
import jax.numpy as jnp
from jax import lax
from jax.sharding import PartitionSpec as P

PASSES = 4


def padded(cells, sides, width, closed):
    for axis, dim in sides:
        count = lax.axis_size(axis)
        ends = count if closed else count - 1
        head = lax.slice_in_dim(cells, 0, width, axis=dim)
        tail = lax.slice_in_dim(cells, cells.shape[dim] - width, cells.shape[dim], axis=dim)
        cells = jnp.concatenate(
            [
                lax.ppermute(tail, axis, [(i, (i + 1) % count) for i in range(ends)]),
                cells,
                lax.ppermute(head, axis, [((i + 1) % count, i) for i in range(ends)]),
            ],
            axis=dim,
        )
    return cells


def smooth(centre, lat_padded, lon_padded, padded_coef):
    middle = padded_coef[1:-1, 1:-1]
    upper_face = (0.5 * (middle + padded_coef[:-2, 1:-1]))[None, :, :, None]
    lower_face = (0.5 * (middle + padded_coef[2:, 1:-1]))[None, :, :, None]
    left_face = (0.5 * (middle + padded_coef[1:-1, :-2]))[None, :, :, None]
    right_face = (0.5 * (middle + padded_coef[1:-1, 2:]))[None, :, :, None]
    return (
        centre
        + upper_face * (lat_padded[:, :-2] - centre)
        + lower_face * (lat_padded[:, 2:] - centre)
        + left_face * (lon_padded[:, :, :-2] - centre)
        + right_face * (lon_padded[:, :, 2:] - centre)
    )


def diffuse_single(field, padded_coef):
    inner_coef = padded_coef[
        PASSES - 1 : padded_coef.shape[0] - PASSES + 1,
        PASSES - 1 : padded_coef.shape[1] - PASSES + 1,
    ]
    for layer_pass in range(PASSES):
        lat_padded = padded(field, (("lat", 1),), 1, False)
        lon_padded = padded(field, (("lon", 2),), 1, True)
        field = smooth(field, lat_padded, lon_padded, inner_coef)
    return field


def vertical_masked(field, region_map, correlation, transpose):
    pattern = "vabl,rvlm->rvabm" if transpose else "vabm,rvlm->rvabl"
    products = jnp.einsum(pattern, field, correlation, precision=lax.Precision.HIGHEST)
    region_ids = jnp.arange(correlation.shape[0], dtype=jnp.int32)
    picked = (region_map[None, :, :] == region_ids[:, None, None]).astype(field.dtype)
    return jnp.sum(products * picked[:, None, :, :, None], axis=0)


def vertical(field, region_map, correlation, transpose):
    return vertical_masked(field, region_map, correlation, transpose)


def on_device(control, observed, deviation, obs_weight, diffusivity, region_map, correlation):
    padded_coef = padded(diffusivity, (("lon", 1),), PASSES, True)
    padded_coef = padded(padded_coef, (("lat", 0),), PASSES, False)
    smoothed = diffuse_single(control, padded_coef)
    state = deviation * vertical(smoothed, region_map, correlation, False)
    weighted = deviation * (obs_weight[None, :, :, None] * (state - observed))
    back = vertical(weighted, region_map, correlation, True)
    spread_back = diffuse_single(back, padded_coef)
    return control + spread_back


def solution(mesh):
    in_specs = (
        P(None, "lat", "lon", None),
        P(None, "lat", "lon", None),
        P(None, "lat", "lon", None),
        P("lat", "lon"),
        P("lat", "lon"),
        P("lat", "lon"),
        P(),
    )
    out_specs = P(None, "lat", "lon", None)
    return jax.shard_map(
        on_device, mesh=mesh, in_specs=in_specs, out_specs=out_specs, check_vma=False
    )
```

profile of v0, /device:TPU:1, one launch (start us, length us, event | category | flops | bytes accessed | tf_op | source)
XLA Modules:
  0.0 186.4 jit_solution(15026583799561515090)
XLA Ops:
  0.0 0.7 fusion.147
  0.7 2.1 %collective-permute-start = (f32[32,4]{0,1:T(4,128)S(1)}, f32[32,4]{0,1:T(4,128)S(1)}, u32[]{:S(2)}, u32[]{:S(2)}) collective-permute-start(f32[32,4]{0,1:T(4,128)S(1)} %get-tuple-element.43), channel_id=1, source_target_pairs={{0,4},{4,8},{8,12},{12,16},{16,20},{20,24},{24,28},{28,32},{32,36}... | collective-permute-start | bytes 1544 | tf_op jit(solution)/shard_map/ppermute | solution.py:17
  2.8 9.2 %collective-permute-start.1 = (f32[32,4]{0,1:T(4,128)S(1)}, f32[32,4]{0,1:T(4,128)S(1)}, u32[]{:S(2)}, u32[]{:S(2)}) collective-permute-start(f32[32,4]{0,1:T(4,128)S(1)} %get-tuple-element.44), channel_id=1, source_target_pairs={{4,0},{8,4},{12,8},{16,12},{20,16},{24,20},{28,24},{32,28},{36,32}... | collective-permute-start | bytes 1544 | tf_op jit(solution)/shard_map/ppermute | solution.py:19
  12.0 1.3 fusion.145
  13.3 0.1 collective-permute-start.6
  13.4 7.2 %collective-permute-start.7 = (f32[4,32,1,128]{3,2,1,0:T(1,128)S(1)}, f32[4,32,1,128]{3,2,1,0:T(1,128)S(1)}, u32[]{:S(2)}, u32[]{:S(2)}) collective-permute-start(f32[4,32,1,128]{3,2,1,0:T(1,128)S(1)} %get-tuple-element.36), channel_id=1, source_target_pairs={{4,0},{8,4},{12,8},{16,12},{20,16},{24,20},{28,24},{32,28},{36,32}... | collective-permute-start | bytes 196616 | tf_op jit(solution)/shard_map/ppermute | solution.py:19
  20.6 0.7 pad_maximum_fusion.32
  21.4 3.6 %collective-permute-start.2 = (f32[4,24]{0,1:T(8,128)S(1)}, f32[4,24]{0,1:T(8,128)S(1)}, u32[]{:S(2)}, u32[]{:S(2)}) collective-permute-start(f32[4,24]{0,1:T(8,128)S(1)} %get-tuple-element.39), channel_id=1, source_target_pairs={{0,1},{1,2},{2,3},{4,5},{5,6},{6,7},{8,9},{9,10},{10,11},{12,13},{... | collective-permute-start | bytes 1160 | tf_op jit(solution)/shard_map/ppermute | solution.py:17
  25.0 1.9 %collective-permute-start.4 = (f32[4,24]{0,1:T(8,128)S(1)}, f32[4,24]{0,1:T(8,128)S(1)}, u32[]{:S(2)}, u32[]{:S(2)}) collective-permute-start(f32[4,24]{0,1:T(8,128)S(1)} %get-tuple-element.40), channel_id=1, source_target_pairs={{1,0},{2,1},{3,2},{5,4},{6,5},{7,6},{9,8},{10,9},{11,10},{13,12},{... | collective-permute-start | bytes 1160 | tf_op jit(solution)/shard_map/ppermute | solution.py:19
  26.9 0.8 fusion.144
  27.7 3.6 %collective-permute-start.3 = (f32[4,1,16,128]{3,2,1,0:T(8,128)S(1)}, f32[4,1,16,128]{3,2,1,0:T(8,128)S(1)}, u32[]{:S(2)}, u32[]{:S(2)}) collective-permute-start(f32[4,1,16,128]{3,2,1,0:T(8,128)S(1)} %get-tuple-element.33), channel_id=1, source_target_pairs={{0,1},{1,2},{2,3},{4,5},{5,6},{6,7},{8,9},{9,10},{10,11},{12,13},{... | collective-permute-start | bytes 98312 | tf_op jit(solution)/shard_map/ppermute | solution.py:17
  31.4 1.9 %collective-permute-start.5 = (f32[4,1,16,128]{3,2,1,0:T(8,128)S(1)}, f32[4,1,16,128]{3,2,1,0:T(8,128)S(1)}, u32[]{:S(2)}, u32[]{:S(2)}) collective-permute-start(f32[4,1,16,128]{3,2,1,0:T(8,128)S(1)} %get-tuple-element.34), channel_id=1, source_target_pairs={{1,0},{2,1},{3,2},{5,4},{6,5},{7,6},{9,8},{10,9},{11,10},{13,12},{... | collective-permute-start | bytes 98312 | tf_op jit(solution)/shard_map/ppermute | solution.py:19
  33.3 1.0 fusion.128
  34.6 2.0 %collective-permute-done.5 = f32[4,1,16,128]{3,2,1,0:T(8,128)S(1)} collective-permute-done((f32[4,1,16,128]{3,2,1,0:T(8,128)S(1)}, f32[4,1,16,128]{3,2,1,0:T(8,128)S(1)}, u32[]{:S(2)}, u32[]{:S(2)}) %collective-permute-start.5) | collective-permute-done | bytes 32800 | tf_op jit(solution)/shard_map/ppermute | solution.py:19
  36.6 3.6 %fusion.100 = f32[4,32,16,128]{3,2,1,0:T(8,128)S(1)} fusion(f32[4,32,16,128]{3,2,1,0:T(8,128)} %param.7, f32[4,32,1,128]{3,2,1,0:T(1,128)S(1)} %collective-permute-done.7, f32[4,32,1,128]{3,2,1,0:T(1,128)S(1)} %collective-permute-done.6, f32[4,1,16,128]{3,2,1,0:T(8,128)S(1)} %collective-permute-done.5, f32[4,1,16,128]{3,2,1,0:T(8,128)S(1)} %collective-permute-done.3, ...), kind=kLoop, calls=%fused_computation.127 | loop fusion | flops 4194304 | bytes 2301952 | tf_op jit(solution)/shard_map/add | solution.py:33
  40.2 0.1 fusion.143
  40.3 0.1 collective-permute-start.10
  40.4 7.2 %collective-permute-start.11 = (f32[4,32,1,128]{3,2,1,0:T(1,128)S(1)}, f32[4,32,1,128]{3,2,1,0:T(1,128)S(1)}, u32[]{:S(2)}, u32[]{:S(2)}) collective-permute-start(f32[4,32,1,128]{3,2,1,0:T(1,128)S(1)} %get-tuple-element.32), channel_id=1, source_target_pairs={{4,0},{8,4},{12,8},{16,12},{20,16},{24,20},{28,24},{32,28},{36,32}... | collective-permute-start | bytes 196616 | tf_op jit(solution)/shard_map/ppermute | solution.py:19
  47.6 2.5 %collective-permute-start.8 = (f32[4,1,16,128]{3,2,1,0:T(8,128)S(1)}, f32[4,1,16,128]{3,2,1,0:T(8,128)S(1)}, u32[]{:S(2)}, u32[]{:S(2)}) collective-permute-start(f32[4,1,16,128]{3,2,1,0:T(8,128)S(1)} %get-tuple-element.29), channel_id=1, source_target_pairs={{0,1},{1,2},{2,3},{4,5},{5,6},{6,7},{8,9},{9,10},{10,11},{12,13},{... | collective-permute-start | bytes 98312 | tf_op jit(solution)/shard_map/ppermute | solution.py:17
  50.0 1.9 %collective-permute-start.9 = (f32[4,1,16,128]{3,2,1,0:T(8,128)S(1)}, f32[4,1,16,128]{3,2,1,0:T(8,128)S(1)}, u32[]{:S(2)}, u32[]{:S(2)}) collective-permute-start(f32[4,1,16,128]{3,2,1,0:T(8,128)S(1)} %get-tuple-element.30), channel_id=1, source_target_pairs={{1,0},{2,1},{3,2},{5,4},{6,5},{7,6},{9,8},{10,9},{11,10},{13,12},{... | collective-permute-start | bytes 98312 | tf_op jit(solution)/shard_map/ppermute | solution.py:19
  52.0 3.3 %collective-permute-done.9 = f32[4,1,16,128]{3,2,1,0:T(8,128)S(1)} collective-permute-done((f32[4,1,16,128]{3,2,1,0:T(8,128)S(1)}, f32[4,1,16,128]{3,2,1,0:T(8,128)S(1)}, u32[]{:S(2)}, u32[]{:S(2)}) %collective-permute-start.9) | collective-permute-done | bytes 32800 | tf_op jit(solution)/shard_map/ppermute | solution.py:19
  55.3 1.1 fusion.88
  56.3 0.1 fusion.141
  56.4 0.1 collective-permute-start.14
  56.5 7.2 %collective-permute-start.15 = (f32[4,32,1,128]{3,2,1,0:T(1,128)S(1)}, f32[4,32,1,128]{3,2,1,0:T(1,128)S(1)}, u32[]{:S(2)}, u32[]{:S(2)}) collective-permute-start(f32[4,32,1,128]{3,2,1,0:T(1,128)S(1)} %get-tuple-element.28), channel_id=1, source_target_pairs={{4,0},{8,4},{12,8},{16,12},{20,16},{24,20},{28,24},{32,28},{36,32}... | collective-permute-start | bytes 196616 | tf_op jit(solution)/shard_map/ppermute | solution.py:19
  63.7 2.5 %collective-permute-start.12 = (f32[4,1,16,128]{3,2,1,0:T(8,128)S(1)}, f32[4,1,16,128]{3,2,1,0:T(8,128)S(1)}, u32[]{:S(2)}, u32[]{:S(2)}) collective-permute-start(f32[4,1,16,128]{3,2,1,0:T(8,128)S(1)} %get-tuple-element.25), channel_id=1, source_target_pairs={{0,1},{1,2},{2,3},{4,5},{5,6},{6,7},{8,9},{9,10},{10,11},{12,13},{... | collective-permute-start | bytes 98312 | tf_op jit(solution)/shard_map/ppermute | solution.py:17
  66.2 1.9 %collective-permute-start.13 = (f32[4,1,16,128]{3,2,1,0:T(8,128)S(1)}, f32[4,1,16,128]{3,2,1,0:T(8,128)S(1)}, u32[]{:S(2)}, u32[]{:S(2)}) collective-permute-start(f32[4,1,16,128]{3,2,1,0:T(8,128)S(1)} %get-tuple-element.26), channel_id=1, source_target_pairs={{1,0},{2,1},{3,2},{5,4},{6,5},{7,6},{9,8},{10,9},{11,10},{13,12},{... | collective-permute-start | bytes 98312 | tf_op jit(solution)/shard_map/ppermute | solution.py:19
  68.2 3.2 %collective-permute-done.13 = f32[4,1,16,128]{3,2,1,0:T(8,128)S(1)} collective-permute-done((f32[4,1,16,128]{3,2,1,0:T(8,128)S(1)}, f32[4,1,16,128]{3,2,1,0:T(8,128)S(1)}, u32[]{:S(2)}, u32[]{:S(2)}) %collective-permute-start.13) | collective-permute-done | bytes 32800 | tf_op jit(solution)/shard_map/ppermute | solution.py:19
  71.4 1.0 fusion.76
  72.5 0.1 fusion.139
  72.6 0.1 collective-permute-start.18
  72.7 7.2 %collective-permute-start.19 = (f32[4,32,1,128]{3,2,1,0:T(1,128)S(1)}, f32[4,32,1,128]{3,2,1,0:T(1,128)S(1)}, u32[]{:S(2)}, u32[]{:S(2)}) collective-permute-start(f32[4,32,1,128]{3,2,1,0:T(1,128)S(1)} %get-tuple-element.24), channel_id=1, source_target_pairs={{4,0},{8,4},{12,8},{16,12},{20,16},{24,20},{28,24},{32,28},{36,32}... | collective-permute-start | bytes 196616 | tf_op jit(solution)/shard_map/ppermute | solution.py:19
  79.8 2.5 %collective-permute-start.16 = (f32[4,1,16,128]{3,2,1,0:T(8,128)S(1)}, f32[4,1,16,128]{3,2,1,0:T(8,128)S(1)}, u32[]{:S(2)}, u32[]{:S(2)}) collective-permute-start(f32[4,1,16,128]{3,2,1,0:T(8,128)S(1)} %get-tuple-element.21), channel_id=1, source_target_pairs={{0,1},{1,2},{2,3},{4,5},{5,6},{6,7},{8,9},{9,10},{10,11},{12,13},{... | collective-permute-start | bytes 98312 | tf_op jit(solution)/shard_map/ppermute | solution.py:17
  82.3 2.1 %collective-permute-start.17 = (f32[4,1,16,128]{3,2,1,0:T(8,128)S(1)}, f32[4,1,16,128]{3,2,1,0:T(8,128)S(1)}, u32[]{:S(2)}, u32[]{:S(2)}) collective-permute-start(f32[4,1,16,128]{3,2,1,0:T(8,128)S(1)} %get-tuple-element.22), channel_id=1, source_target_pairs={{1,0},{2,1},{3,2},{5,4},{6,5},{7,6},{9,8},{10,9},{11,10},{13,12},{... | collective-permute-start | bytes 98312 | tf_op jit(solution)/shard_map/ppermute | solution.py:19
  84.6 3.0 %collective-permute-done.17 = f32[4,1,16,128]{3,2,1,0:T(8,128)S(1)} collective-permute-done((f32[4,1,16,128]{3,2,1,0:T(8,128)S(1)}, f32[4,1,16,128]{3,2,1,0:T(8,128)S(1)}, u32[]{:S(2)}, u32[]{:S(2)}) %collective-permute-start.17) | collective-permute-done | bytes 32800 | tf_op jit(solution)/shard_map/ppermute | solution.py:19
  87.6 17.1 %fusion.1 = f32[4,32,16,128]{3,2,1,0:T(8,128)S(1)} fusion(f32[16,32,16]{2,0,1:T(8,128)S(1)} %fusion.120, f32[4,32,16,128]{3,2,1,0:T(8,128)S(1)} %fusion.76, f32[4,32,1,128]{3,2,1,0:T(1,128)S(1)} %collective-permute-done.19, f32[4,32,1,128]{3,2,1,0:T(1,128)S(1)} %collective-permute-done.18, f32[4,1,16,128]{3,2,1,0:T(8,128)S(1)} %collective-permute-done.17, ...), kind=kOutput, calls=%fused_computation.3 | convolution fusion | flops 6454771712 | bytes 6529024 | tf_op jit(solution)/shard_map/vabm,rvlm->rvabl/dot_general | solution.py:55
  104.6 15.4 %fusion = f32[4,32,16,128]{3,2,1,0:T(8,128)S(1)} fusion(f32[16,32,16]{2,0,1:T(8,128)S(1)} %fusion.120, f32[4,32,16,128]{3,2,1,0:T(8,128)S(1)} %copy-done.4, f32[4,32,16,128]{3,2,1,0:T(8,128)S(1)} %copy-done.5, f32[4,32,16,128]{3,2,1,0:T(8,128)S(1)} %fusion.1, f32[32,16]{1,0:T(8,128)S(1)} %copy.8, f32[16,4,128,128]{3,2,1,0:T(8,128)S(1)} %copy-done.3), kind=kOutput, calls=%fused_computation.1 | convolution fusion | flops 6451625984 | bytes 8423424 | tf_op jit(solution)/shard_map/vabl,rvlm->rvabm/dot_general | solution.py:55
  120.1 0.1 fusion.137
  120.2 0.3 collective-permute-start.22
  120.5 7.2 %collective-permute-start.23 = (f32[4,32,1,128]{3,2,1,0:T(1,128)S(1)}, f32[4,32,1,128]{3,2,1,0:T(1,128)S(1)}, u32[]{:S(2)}, u32[]{:S(2)}) collective-permute-start(f32[4,32,1,128]{3,2,1,0:T(1,128)S(1)} %get-tuple-element.20), channel_id=1, source_target_pairs={{4,0},{8,4},{12,8},{16,12},{20,16},{24,20},{28,24},{32,28},{36,32}... | collective-permute-start | bytes 196616 | tf_op jit(solution)/shard_map/ppermute | solution.py:19
  127.7 3.0 %collective-permute-start.20 = (f32[4,1,16,128]{3,2,1,0:T(8,128)S(1)}, f32[4,1,16,128]{3,2,1,0:T(8,128)S(1)}, u32[]{:S(2)}, u32[]{:S(2)}) collective-permute-start(f32[4,1,16,128]{3,2,1,0:T(8,128)S(1)} %get-tuple-element.17), channel_id=1, source_target_pairs={{0,1},{1,2},{2,3},{4,5},{5,6},{6,7},{8,9},{9,10},{10,11},{12,13},{... | collective-permute-start | bytes 98312 | tf_op jit(solution)/shard_map/ppermute | solution.py:17
  130.6 1.9 %collective-permute-start.21 = (f32[4,1,16,128]{3,2,1,0:T(8,128)S(1)}, f32[4,1,16,128]{3,2,1,0:T(8,128)S(1)}, u32[]{:S(2)}, u32[]{:S(2)}) collective-permute-start(f32[4,1,16,128]{3,2,1,0:T(8,128)S(1)} %get-tuple-element.18), channel_id=1, source_target_pairs={{1,0},{2,1},{3,2},{5,4},{6,5},{7,6},{9,8},{10,9},{11,10},{13,12},{... | collective-permute-start | bytes 98312 | tf_op jit(solution)/shard_map/ppermute | solution.py:19
  132.6 3.3 %collective-permute-done.21 = f32[4,1,16,128]{3,2,1,0:T(8,128)S(1)} collective-permute-done((f32[4,1,16,128]{3,2,1,0:T(8,128)S(1)}, f32[4,1,16,128]{3,2,1,0:T(8,128)S(1)}, u32[]{:S(2)}, u32[]{:S(2)}) %collective-permute-start.21) | collective-permute-done | bytes 32800 | tf_op jit(solution)/shard_map/ppermute | solution.py:19
  135.9 1.0 fusion.43
  136.9 0.1 fusion.135
  137.0 0.1 collective-permute-start.26
  137.1 7.2 %collective-permute-start.27 = (f32[4,32,1,128]{3,2,1,0:T(1,128)S(1)}, f32[4,32,1,128]{3,2,1,0:T(1,128)S(1)}, u32[]{:S(2)}, u32[]{:S(2)}) collective-permute-start(f32[4,32,1,128]{3,2,1,0:T(1,128)S(1)} %get-tuple-element.16), channel_id=1, source_target_pairs={{4,0},{8,4},{12,8},{16,12},{20,16},{24,20},{28,24},{32,28},{36,32}... | collective-permute-start | bytes 196616 | tf_op jit(solution)/shard_map/ppermute | solution.py:19
  144.3 2.5 %collective-permute-start.24 = (f32[4,1,16,128]{3,2,1,0:T(8,128)S(1)}, f32[4,1,16,128]{3,2,1,0:T(8,128)S(1)}, u32[]{:S(2)}, u32[]{:S(2)}) collective-permute-start(f32[4,1,16,128]{3,2,1,0:T(8,128)S(1)} %get-tuple-element.13), channel_id=1, source_target_pairs={{0,1},{1,2},{2,3},{4,5},{5,6},{6,7},{8,9},{9,10},{10,11},{12,13},{... | collective-permute-start | bytes 98312 | tf_op jit(solution)/shard_map/ppermute | solution.py:17
  146.8 1.9 %collective-permute-start.25 = (f32[4,1,16,128]{3,2,1,0:T(8,128)S(1)}, f32[4,1,16,128]{3,2,1,0:T(8,128)S(1)}, u32[]{:S(2)}, u32[]{:S(2)}) collective-permute-start(f32[4,1,16,128]{3,2,1,0:T(8,128)S(1)} %get-tuple-element.14), channel_id=1, source_target_pairs={{1,0},{2,1},{3,2},{5,4},{6,5},{7,6},{9,8},{10,9},{11,10},{13,12},{... | collective-permute-start | bytes 98312 | tf_op jit(solution)/shard_map/ppermute | solution.py:19
  148.7 4.0 %collective-permute-done.25 = f32[4,1,16,128]{3,2,1,0:T(8,128)S(1)} collective-permute-done((f32[4,1,16,128]{3,2,1,0:T(8,128)S(1)}, f32[4,1,16,128]{3,2,1,0:T(8,128)S(1)}, u32[]{:S(2)}, u32[]{:S(2)}) %collective-permute-start.25) | collective-permute-done | bytes 32800 | tf_op jit(solution)/shard_map/ppermute | solution.py:19
  152.7 1.1 fusion.31
  153.8 0.1 fusion.133
  153.9 0.1 collective-permute-start.30
  154.0 7.2 %collective-permute-start.31 = (f32[4,32,1,128]{3,2,1,0:T(1,128)S(1)}, f32[4,32,1,128]{3,2,1,0:T(1,128)S(1)}, u32[]{:S(2)}, u32[]{:S(2)}) collective-permute-start(f32[4,32,1,128]{3,2,1,0:T(1,128)S(1)} %get-tuple-element.12), channel_id=1, source_target_pairs={{4,0},{8,4},{12,8},{16,12},{20,16},{24,20},{28,24},{32,28},{36,32}... | collective-permute-start | bytes 196616 | tf_op jit(solution)/shard_map/ppermute | solution.py:19
  161.1 1.9 %collective-permute-start.28 = (f32[4,1,16,128]{3,2,1,0:T(8,128)S(1)}, f32[4,1,16,128]{3,2,1,0:T(8,128)S(1)}, u32[]{:S(2)}, u32[]{:S(2)}) collective-permute-start(f32[4,1,16,128]{3,2,1,0:T(8,128)S(1)} %get-tuple-element.9), channel_id=1, source_target_pairs={{0,1},{1,2},{2,3},{4,5},{5,6},{6,7},{8,9},{9,10},{10,11},{12,13},{... | collective-permute-start | bytes 98312 | tf_op jit(solution)/shard_map/ppermute | solution.py:17
  163.1 2.4 %collective-permute-start.29 = (f32[4,1,16,128]{3,2,1,0:T(8,128)S(1)}, f32[4,1,16,128]{3,2,1,0:T(8,128)S(1)}, u32[]{:S(2)}, u32[]{:S(2)}) collective-permute-start(f32[4,1,16,128]{3,2,1,0:T(8,128)S(1)} %get-tuple-element.10), channel_id=1, source_target_pairs={{1,0},{2,1},{3,2},{5,4},{6,5},{7,6},{9,8},{10,9},{11,10},{13,12},{... | collective-permute-start | bytes 98312 | tf_op jit(solution)/shard_map/ppermute | solution.py:19
  165.5 2.8 %collective-permute-done.29 = f32[4,1,16,128]{3,2,1,0:T(8,128)S(1)} collective-permute-done((f32[4,1,16,128]{3,2,1,0:T(8,128)S(1)}, f32[4,1,16,128]{3,2,1,0:T(8,128)S(1)}, u32[]{:S(2)}, u32[]{:S(2)}) %collective-permute-start.29) | collective-permute-done | bytes 32800 | tf_op jit(solution)/shard_map/ppermute | solution.py:19
  168.3 1.1 fusion.19
  169.4 0.1 fusion.131
  169.6 7.2 %collective-permute-start.35 = (f32[4,32,1,128]{3,2,1,0:T(1,128)S(1)}, f32[4,32,1,128]{3,2,1,0:T(1,128)S(1)}, u32[]{:S(2)}, u32[]{:S(2)}) collective-permute-start(f32[4,32,1,128]{3,2,1,0:T(1,128)S(1)} %get-tuple-element.8), channel_id=1, source_target_pairs={{4,0},{8,4},{12,8},{16,12},{20,16},{24,20},{28,24},{32,28},{36,32}... | collective-permute-start | bytes 196616 | tf_op jit(solution)/shard_map/ppermute | solution.py:19
  176.7 2.5 %collective-permute-start.32 = (f32[4,1,16,128]{3,2,1,0:T(8,128)S(1)}, f32[4,1,16,128]{3,2,1,0:T(8,128)S(1)}, u32[]{:S(2)}, u32[]{:S(2)}) collective-permute-start(f32[4,1,16,128]{3,2,1,0:T(8,128)S(1)} %get-tuple-element.5), channel_id=1, source_target_pairs={{0,1},{1,2},{2,3},{4,5},{5,6},{6,7},{8,9},{9,10},{10,11},{12,13},{... | collective-permute-start | bytes 98312 | tf_op jit(solution)/shard_map/ppermute | solution.py:17
  179.2 1.9 %collective-permute-start.33 = (f32[4,1,16,128]{3,2,1,0:T(8,128)S(1)}, f32[4,1,16,128]{3,2,1,0:T(8,128)S(1)}, u32[]{:S(2)}, u32[]{:S(2)}) collective-permute-start(f32[4,1,16,128]{3,2,1,0:T(8,128)S(1)} %get-tuple-element.6), channel_id=1, source_target_pairs={{1,0},{2,1},{3,2},{5,4},{6,5},{7,6},{9,8},{10,9},{11,10},{13,12},{... | collective-permute-start | bytes 98312 | tf_op jit(solution)/shard_map/ppermute | solution.py:19
  181.1 3.3 %collective-permute-done.33 = f32[4,1,16,128]{3,2,1,0:T(8,128)S(1)} collective-permute-done((f32[4,1,16,128]{3,2,1,0:T(8,128)S(1)}, f32[4,1,16,128]{3,2,1,0:T(8,128)S(1)}, u32[]{:S(2)}, u32[]{:S(2)}) %collective-permute-start.33) | collective-permute-done | bytes 32800 | tf_op jit(solution)/shard_map/ppermute | solution.py:19
  184.4 2.0 %fusion.7 = f32[4,32,16,128]{3,2,1,0:T(8,128)} fusion(f32[4,32,16,128]{3,2,1,0:T(8,128)S(1)} %copy-done, f32[4,32,16,128]{3,2,1,0:T(8,128)S(1)} %fusion.19, f32[4,32,1,128]{3,2,1,0:T(1,128)S(1)} %collective-permute-done.35, f32[4,32,1,128]{3,2,1,0:T(1,128)S(1)} %collective-permute-done.34, f32[4,1,16,128]{3,2,1,0:T(8,128)S(1)} %collective-permute-done.33, ...), kind=kLoop, calls=%fused_computation.10 | loop fusion | flops 4456448 | bytes 3350528 | tf_op jit(solution)/shard_map/add | solution.py:73
  (56 shorter events, 0.8 us)
Async XLA Ops:
  0.0 68.1 %copy-start.1 = (s32[32,16]{0,1:T(8,128)S(1)}, s32[32,16]{0,1:T(8,128)}, u32[]{:S(2)}) copy-start(s32[32,16]{0,1:T(8,128)} %param.12) | copy-start | bytes 6148
  0.7 19.9 %collective-permute-start = (f32[32,4]{0,1:T(4,128)S(1)}, f32[32,4]{0,1:T(4,128)S(1)}, u32[]{:S(2)}, u32[]{:S(2)}) collective-permute-start(f32[32,4]{0,1:T(4,128)S(1)} %get-tuple-element.43), channel_id=1, source_target_pairs={{0,4},{4,8},{8,12},{12,16},{16,20},{20,24},{24,28},{28,32},{32,36}... | collective-permute-start | bytes 1544 | tf_op jit(solution)/shard_map/ppermute | solution.py:17
  2.8 17.8 %collective-permute-start.1 = (f32[32,4]{0,1:T(4,128)S(1)}, f32[32,4]{0,1:T(4,128)S(1)}, u32[]{:S(2)}, u32[]{:S(2)}) collective-permute-start(f32[32,4]{0,1:T(4,128)S(1)} %get-tuple-element.44), channel_id=1, source_target_pairs={{4,0},{8,4},{12,8},{16,12},{20,16},{24,20},{28,24},{32,28},{36,32}... | collective-permute-start | bytes 1544 | tf_op jit(solution)/shard_map/ppermute | solution.py:19
  13.3 23.3 %collective-permute-start.6 = (f32[4,32,1,128]{3,2,1,0:T(1,128)S(1)}, f32[4,32,1,128]{3,2,1,0:T(1,128)S(1)}, u32[]{:S(2)}, u32[]{:S(2)}) collective-permute-start(f32[4,32,1,128]{3,2,1,0:T(1,128)S(1)} %get-tuple-element.35), channel_id=1, source_target_pairs={{0,4},{4,8},{8,12},{12,16},{16,20},{20,24},{24,28},{28,32},{32,36}... | collective-permute-start | bytes 196616 | tf_op jit(solution)/shard_map/ppermute | solution.py:17
  13.4 23.2 %collective-permute-start.7 = (f32[4,32,1,128]{3,2,1,0:T(1,128)S(1)}, f32[4,32,1,128]{3,2,1,0:T(1,128)S(1)}, u32[]{:S(2)}, u32[]{:S(2)}) collective-permute-start(f32[4,32,1,128]{3,2,1,0:T(1,128)S(1)} %get-tuple-element.36), channel_id=1, source_target_pairs={{4,0},{8,4},{12,8},{16,12},{20,16},{24,20},{28,24},{32,28},{36,32}... | collective-permute-start | bytes 196616 | tf_op jit(solution)/shard_map/ppermute | solution.py:19
  21.4 10.0 %collective-permute-start.2 = (f32[4,24]{0,1:T(8,128)S(1)}, f32[4,24]{0,1:T(8,128)S(1)}, u32[]{:S(2)}, u32[]{:S(2)}) collective-permute-start(f32[4,24]{0,1:T(8,128)S(1)} %get-tuple-element.39), channel_id=1, source_target_pairs={{0,1},{1,2},{2,3},{4,5},{5,6},{6,7},{8,9},{9,10},{10,11},{12,13},{... | collective-permute-start | bytes 1160 | tf_op jit(solution)/shard_map/ppermute | solution.py:17
  25.0 8.3 %collective-permute-start.4 = (f32[4,24]{0,1:T(8,128)S(1)}, f32[4,24]{0,1:T(8,128)S(1)}, u32[]{:S(2)}, u32[]{:S(2)}) collective-permute-start(f32[4,24]{0,1:T(8,128)S(1)} %get-tuple-element.40), channel_id=1, source_target_pairs={{1,0},{2,1},{3,2},{5,4},{6,5},{7,6},{9,8},{10,9},{11,10},{13,12},{... | collective-permute-start | bytes 1160 | tf_op jit(solution)/shard_map/ppermute | solution.py:19
  27.7 6.9 %collective-permute-start.3 = (f32[4,1,16,128]{3,2,1,0:T(8,128)S(1)}, f32[4,1,16,128]{3,2,1,0:T(8,128)S(1)}, u32[]{:S(2)}, u32[]{:S(2)}) collective-permute-start(f32[4,1,16,128]{3,2,1,0:T(8,128)S(1)} %get-tuple-element.33), channel_id=1, source_target_pairs={{0,1},{1,2},{2,3},{4,5},{5,6},{6,7},{8,9},{9,10},{10,11},{12,13},{... | collective-permute-start | bytes 98312 | tf_op jit(solution)/shard_map/ppermute | solution.py:17
  31.4 5.2 %collective-permute-start.5 = (f32[4,1,16,128]{3,2,1,0:T(8,128)S(1)}, f32[4,1,16,128]{3,2,1,0:T(8,128)S(1)}, u32[]{:S(2)}, u32[]{:S(2)}) collective-permute-start(f32[4,1,16,128]{3,2,1,0:T(8,128)S(1)} %get-tuple-element.34), channel_id=1, source_target_pairs={{1,0},{2,1},{3,2},{5,4},{6,5},{7,6},{9,8},{10,9},{11,10},{13,12},{... | collective-permute-start | bytes 98312 | tf_op jit(solution)/shard_map/ppermute | solution.py:19
  34.6 49.9 %copy-start.2 = (f32[32,16]{0,1:T(8,128)S(1)}, f32[32,16]{0,1:T(8,128)}, u32[]{:S(2)}) copy-start(f32[32,16]{0,1:T(8,128)} %param.10) | copy-start | bytes 6148
  40.3 15.0 %collective-permute-start.10 = (f32[4,32,1,128]{3,2,1,0:T(1,128)S(1)}, f32[4,32,1,128]{3,2,1,0:T(1,128)S(1)}, u32[]{:S(2)}, u32[]{:S(2)}) collective-permute-start(f32[4,32,1,128]{3,2,1,0:T(1,128)S(1)} %get-tuple-element.31), channel_id=1, source_target_pairs={{0,4},{4,8},{8,12},{12,16},{16,20},{20,24},{24,28},{28,32},{32,36}... | collective-permute-start | bytes 196616 | tf_op jit(solution)/shard_map/ppermute | solution.py:17
  40.4 14.9 %collective-permute-start.11 = (f32[4,32,1,128]{3,2,1,0:T(1,128)S(1)}, f32[4,32,1,128]{3,2,1,0:T(1,128)S(1)}, u32[]{:S(2)}, u32[]{:S(2)}) collective-permute-start(f32[4,32,1,128]{3,2,1,0:T(1,128)S(1)} %get-tuple-element.32), channel_id=1, source_target_pairs={{4,0},{8,4},{12,8},{16,12},{20,16},{24,20},{28,24},{32,28},{36,32}... | collective-permute-start | bytes 196616 | tf_op jit(solution)/shard_map/ppermute | solution.py:19
  47.6 4.4 %collective-permute-start.8 = (f32[4,1,16,128]{3,2,1,0:T(8,128)S(1)}, f32[4,1,16,128]{3,2,1,0:T(8,128)S(1)}, u32[]{:S(2)}, u32[]{:S(2)}) collective-permute-start(f32[4,1,16,128]{3,2,1,0:T(8,128)S(1)} %get-tuple-element.29), channel_id=1, source_target_pairs={{0,1},{1,2},{2,3},{4,5},{5,6},{6,7},{8,9},{9,10},{10,11},{12,13},{... | collective-permute-start | bytes 98312 | tf_op jit(solution)/shard_map/ppermute | solution.py:17
  50.0 5.2 %collective-permute-start.9 = (f32[4,1,16,128]{3,2,1,0:T(8,128)S(1)}, f32[4,1,16,128]{3,2,1,0:T(8,128)S(1)}, u32[]{:S(2)}, u32[]{:S(2)}) collective-permute-start(f32[4,1,16,128]{3,2,1,0:T(8,128)S(1)} %get-tuple-element.30), channel_id=1, source_target_pairs={{1,0},{2,1},{3,2},{5,4},{6,5},{7,6},{9,8},{10,9},{11,10},{13,12},{... | collective-permute-start | bytes 98312 | tf_op jit(solution)/shard_map/ppermute | solution.py:19
  56.4 15.0 %collective-permute-start.14 = (f32[4,32,1,128]{3,2,1,0:T(1,128)S(1)}, f32[4,32,1,128]{3,2,1,0:T(1,128)S(1)}, u32[]{:S(2)}, u32[]{:S(2)}) collective-permute-start(f32[4,32,1,128]{3,2,1,0:T(1,128)S(1)} %get-tuple-element.27), channel_id=1, source_target_pairs={{0,4},{4,8},{8,12},{12,16},{16,20},{20,24},{24,28},{28,32},{32,36}... | collective-permute-start | bytes 196616 | tf_op jit(solution)/shard_map/ppermute | solution.py:17
  56.5 14.9 %collective-permute-start.15 = (f32[4,32,1,128]{3,2,1,0:T(1,128)S(1)}, f32[4,32,1,128]{3,2,1,0:T(1,128)S(1)}, u32[]{:S(2)}, u32[]{:S(2)}) collective-permute-start(f32[4,32,1,128]{3,2,1,0:T(1,128)S(1)} %get-tuple-element.28), channel_id=1, source_target_pairs={{4,0},{8,4},{12,8},{16,12},{20,16},{24,20},{28,24},{32,28},{36,32}... | collective-permute-start | bytes 196616 | tf_op jit(solution)/shard_map/ppermute | solution.py:19
  63.7 4.5 %collective-permute-start.12 = (f32[4,1,16,128]{3,2,1,0:T(8,128)S(1)}, f32[4,1,16,128]{3,2,1,0:T(8,128)S(1)}, u32[]{:S(2)}, u32[]{:S(2)}) collective-permute-start(f32[4,1,16,128]{3,2,1,0:T(8,128)S(1)} %get-tuple-element.25), channel_id=1, source_target_pairs={{0,1},{1,2},{2,3},{4,5},{5,6},{6,7},{8,9},{9,10},{10,11},{12,13},{... | collective-permute-start | bytes 98312 | tf_op jit(solution)/shard_map/ppermute | solution.py:17
  66.2 5.2 %collective-permute-start.13 = (f32[4,1,16,128]{3,2,1,0:T(8,128)S(1)}, f32[4,1,16,128]{3,2,1,0:T(8,128)S(1)}, u32[]{:S(2)}, u32[]{:S(2)}) collective-permute-start(f32[4,1,16,128]{3,2,1,0:T(8,128)S(1)} %get-tuple-element.26), channel_id=1, source_target_pairs={{1,0},{2,1},{3,2},{5,4},{6,5},{7,6},{9,8},{10,9},{11,10},{13,12},{... | collective-permute-start | bytes 98312 | tf_op jit(solution)/shard_map/ppermute | solution.py:19
  72.6 15.0 %collective-permute-start.18 = (f32[4,32,1,128]{3,2,1,0:T(1,128)S(1)}, f32[4,32,1,128]{3,2,1,0:T(1,128)S(1)}, u32[]{:S(2)}, u32[]{:S(2)}) collective-permute-start(f32[4,32,1,128]{3,2,1,0:T(1,128)S(1)} %get-tuple-element.23), channel_id=1, source_target_pairs={{0,4},{4,8},{8,12},{12,16},{16,20},{20,24},{24,28},{28,32},{32,36}... | collective-permute-start | bytes 196616 | tf_op jit(solution)/shard_map/ppermute | solution.py:17
  72.7 14.9 %collective-permute-start.19 = (f32[4,32,1,128]{3,2,1,0:T(1,128)S(1)}, f32[4,32,1,128]{3,2,1,0:T(1,128)S(1)}, u32[]{:S(2)}, u32[]{:S(2)}) collective-permute-start(f32[4,32,1,128]{3,2,1,0:T(1,128)S(1)} %get-tuple-element.24), channel_id=1, source_target_pairs={{4,0},{8,4},{12,8},{16,12},{20,16},{24,20},{28,24},{32,28},{36,32}... | collective-permute-start | bytes 196616 | tf_op jit(solution)/shard_map/ppermute | solution.py:19
  79.8 4.7 %collective-permute-start.16 = (f32[4,1,16,128]{3,2,1,0:T(8,128)S(1)}, f32[4,1,16,128]{3,2,1,0:T(8,128)S(1)}, u32[]{:S(2)}, u32[]{:S(2)}) collective-permute-start(f32[4,1,16,128]{3,2,1,0:T(8,128)S(1)} %get-tuple-element.21), channel_id=1, source_target_pairs={{0,1},{1,2},{2,3},{4,5},{5,6},{6,7},{8,9},{9,10},{10,11},{12,13},{... | collective-permute-start | bytes 98312 | tf_op jit(solution)/shard_map/ppermute | solution.py:17
  82.3 5.2 %collective-permute-start.17 = (f32[4,1,16,128]{3,2,1,0:T(8,128)S(1)}, f32[4,1,16,128]{3,2,1,0:T(8,128)S(1)}, u32[]{:S(2)}, u32[]{:S(2)}) collective-permute-start(f32[4,1,16,128]{3,2,1,0:T(8,128)S(1)} %get-tuple-element.22), channel_id=1, source_target_pairs={{1,0},{2,1},{3,2},{5,4},{6,5},{7,6},{9,8},{10,9},{11,10},{13,12},{... | collective-permute-start | bytes 98312 | tf_op jit(solution)/shard_map/ppermute | solution.py:19
  84.5 20.1 %copy-start.3 = (f32[16,4,128,128]{3,2,1,0:T(8,128)S(1)}, f32[16,4,128,128]{3,2,1,0:T(8,128)}, u32[]{:S(2)}) copy-start(f32[16,4,128,128]{3,2,1,0:T(8,128)} %param.13) | copy-start | bytes 12582916
  84.5 20.1 %copy-start.4 = (f32[4,32,16,128]{3,2,1,0:T(8,128)S(1)}, f32[4,32,16,128]{3,2,1,0:T(8,128)}, u32[]{:S(2)}) copy-start(f32[4,32,16,128]{3,2,1,0:T(8,128)} %param.9) | copy-start | bytes 3145732
  84.5 20.1 %copy-start.5 = (f32[4,32,16,128]{3,2,1,0:T(8,128)S(1)}, f32[4,32,16,128]{3,2,1,0:T(8,128)}, u32[]{:S(2)}) copy-start(f32[4,32,16,128]{3,2,1,0:T(8,128)} %param.8) | copy-start | bytes 3145732
  120.2 15.7 %collective-permute-start.22 = (f32[4,32,1,128]{3,2,1,0:T(1,128)S(1)}, f32[4,32,1,128]{3,2,1,0:T(1,128)S(1)}, u32[]{:S(2)}, u32[]{:S(2)}) collective-permute-start(f32[4,32,1,128]{3,2,1,0:T(1,128)S(1)} %get-tuple-element.19), channel_id=1, source_target_pairs={{0,4},{4,8},{8,12},{12,16},{16,20},{20,24},{24,28},{28,32},{32,36}... | collective-permute-start | bytes 196616 | tf_op jit(solution)/shard_map/ppermute | solution.py:17
  120.5 64.0 %copy-start = (f32[4,32,16,128]{3,2,1,0:T(8,128)S(1)}, f32[4,32,16,128]{3,2,1,0:T(8,128)}, u32[]{:S(2)}) copy-start(f32[4,32,16,128]{3,2,1,0:T(8,128)} %param.7) | copy-start | bytes 3145732
  120.5 15.4 %collective-permute-start.23 = (f32[4,32,1,128]{3,2,1,0:T(1,128)S(1)}, f32[4,32,1,128]{3,2,1,0:T(1,128)S(1)}, u32[]{:S(2)}, u32[]{:S(2)}) collective-permute-start(f32[4,32,1,128]{3,2,1,0:T(1,128)S(1)} %get-tuple-element.20), channel_id=1, source_target_pairs={{4,0},{8,4},{12,8},{16,12},{20,16},{24,20},{28,24},{32,28},{36,32}... | collective-permute-start | bytes 196616 | tf_op jit(solution)/shard_map/ppermute | solution.py:19
  127.7 4.9 %collective-permute-start.20 = (f32[4,1,16,128]{3,2,1,0:T(8,128)S(1)}, f32[4,1,16,128]{3,2,1,0:T(8,128)S(1)}, u32[]{:S(2)}, u32[]{:S(2)}) collective-permute-start(f32[4,1,16,128]{3,2,1,0:T(8,128)S(1)} %get-tuple-element.17), channel_id=1, source_target_pairs={{0,1},{1,2},{2,3},{4,5},{5,6},{6,7},{8,9},{9,10},{10,11},{12,13},{... | collective-permute-start | bytes 98312 | tf_op jit(solution)/shard_map/ppermute | solution.py:17
  130.6 5.2 %collective-permute-start.21 = (f32[4,1,16,128]{3,2,1,0:T(8,128)S(1)}, f32[4,1,16,128]{3,2,1,0:T(8,128)S(1)}, u32[]{:S(2)}, u32[]{:S(2)}) collective-permute-start(f32[4,1,16,128]{3,2,1,0:T(8,128)S(1)} %get-tuple-element.18), channel_id=1, source_target_pairs={{1,0},{2,1},{3,2},{5,4},{6,5},{7,6},{9,8},{10,9},{11,10},{13,12},{... | collective-permute-start | bytes 98312 | tf_op jit(solution)/shard_map/ppermute | solution.py:19
  137.0 15.7 %collective-permute-start.26 = (f32[4,32,1,128]{3,2,1,0:T(1,128)S(1)}, f32[4,32,1,128]{3,2,1,0:T(1,128)S(1)}, u32[]{:S(2)}, u32[]{:S(2)}) collective-permute-start(f32[4,32,1,128]{3,2,1,0:T(1,128)S(1)} %get-tuple-element.15), channel_id=1, source_target_pairs={{0,4},{4,8},{8,12},{12,16},{16,20},{20,24},{24,28},{28,32},{32,36}... | collective-permute-start | bytes 196616 | tf_op jit(solution)/shard_map/ppermute | solution.py:17
  137.1 15.6 %collective-permute-start.27 = (f32[4,32,1,128]{3,2,1,0:T(1,128)S(1)}, f32[4,32,1,128]{3,2,1,0:T(1,128)S(1)}, u32[]{:S(2)}, u32[]{:S(2)}) collective-permute-start(f32[4,32,1,128]{3,2,1,0:T(1,128)S(1)} %get-tuple-element.16), channel_id=1, source_target_pairs={{4,0},{8,4},{12,8},{16,12},{20,16},{24,20},{28,24},{32,28},{36,32}... | collective-permute-start | bytes 196616 | tf_op jit(solution)/shard_map/ppermute | solution.py:19
  144.3 4.4 %collective-permute-start.24 = (f32[4,1,16,128]{3,2,1,0:T(8,128)S(1)}, f32[4,1,16,128]{3,2,1,0:T(8,128)S(1)}, u32[]{:S(2)}, u32[]{:S(2)}) collective-permute-start(f32[4,1,16,128]{3,2,1,0:T(8,128)S(1)} %get-tuple-element.13), channel_id=1, source_target_pairs={{0,1},{1,2},{2,3},{4,5},{5,6},{6,7},{8,9},{9,10},{10,11},{12,13},{... | collective-permute-start | bytes 98312 | tf_op jit(solution)/shard_map/ppermute | solution.py:17
  146.8 5.9 %collective-permute-start.25 = (f32[4,1,16,128]{3,2,1,0:T(8,128)S(1)}, f32[4,1,16,128]{3,2,1,0:T(8,128)S(1)}, u32[]{:S(2)}, u32[]{:S(2)}) collective-permute-start(f32[4,1,16,128]{3,2,1,0:T(8,128)S(1)} %get-tuple-element.14), channel_id=1, source_target_pairs={{1,0},{2,1},{3,2},{5,4},{6,5},{7,6},{9,8},{10,9},{11,10},{13,12},{... | collective-permute-start | bytes 98312 | tf_op jit(solution)/shard_map/ppermute | solution.py:19
  153.9 14.4 %collective-permute-start.30 = (f32[4,32,1,128]{3,2,1,0:T(1,128)S(1)}, f32[4,32,1,128]{3,2,1,0:T(1,128)S(1)}, u32[]{:S(2)}, u32[]{:S(2)}) collective-permute-start(f32[4,32,1,128]{3,2,1,0:T(1,128)S(1)} %get-tuple-element.11), channel_id=1, source_target_pairs={{0,4},{4,8},{8,12},{12,16},{16,20},{20,24},{24,28},{28,32},{32,36}... | collective-permute-start | bytes 196616 | tf_op jit(solution)/shard_map/ppermute | solution.py:17
  154.0 14.3 %collective-permute-start.31 = (f32[4,32,1,128]{3,2,1,0:T(1,128)S(1)}, f32[4,32,1,128]{3,2,1,0:T(1,128)S(1)}, u32[]{:S(2)}, u32[]{:S(2)}) collective-permute-start(f32[4,32,1,128]{3,2,1,0:T(1,128)S(1)} %get-tuple-element.12), channel_id=1, source_target_pairs={{4,0},{8,4},{12,8},{16,12},{20,16},{24,20},{28,24},{32,28},{36,32}... | collective-permute-start | bytes 196616 | tf_op jit(solution)/shard_map/ppermute | solution.py:19
  161.1 4.3 %collective-permute-start.28 = (f32[4,1,16,128]{3,2,1,0:T(8,128)S(1)}, f32[4,1,16,128]{3,2,1,0:T(8,128)S(1)}, u32[]{:S(2)}, u32[]{:S(2)}) collective-permute-start(f32[4,1,16,128]{3,2,1,0:T(8,128)S(1)} %get-tuple-element.9), channel_id=1, source_target_pairs={{0,1},{1,2},{2,3},{4,5},{5,6},{6,7},{8,9},{9,10},{10,11},{12,13},{... | collective-permute-start | bytes 98312 | tf_op jit(solution)/shard_map/ppermute | solution.py:17
  163.1 5.2 %collective-permute-start.29 = (f32[4,1,16,128]{3,2,1,0:T(8,128)S(1)}, f32[4,1,16,128]{3,2,1,0:T(8,128)S(1)}, u32[]{:S(2)}, u32[]{:S(2)}) collective-permute-start(f32[4,1,16,128]{3,2,1,0:T(8,128)S(1)} %get-tuple-element.10), channel_id=1, source_target_pairs={{1,0},{2,1},{3,2},{5,4},{6,5},{7,6},{9,8},{10,9},{11,10},{13,12},{... | collective-permute-start | bytes 98312 | tf_op jit(solution)/shard_map/ppermute | solution.py:19
  169.5 15.0 %collective-permute-start.34 = (f32[4,32,1,128]{3,2,1,0:T(1,128)S(1)}, f32[4,32,1,128]{3,2,1,0:T(1,128)S(1)}, u32[]{:S(2)}, u32[]{:S(2)}) collective-permute-start(f32[4,32,1,128]{3,2,1,0:T(1,128)S(1)} %get-tuple-element.7), channel_id=1, source_target_pairs={{0,4},{4,8},{8,12},{12,16},{16,20},{20,24},{24,28},{28,32},{32,36}... | collective-permute-start | bytes 196616 | tf_op jit(solution)/shard_map/ppermute | solution.py:17
  169.6 14.9 %collective-permute-start.35 = (f32[4,32,1,128]{3,2,1,0:T(1,128)S(1)}, f32[4,32,1,128]{3,2,1,0:T(1,128)S(1)}, u32[]{:S(2)}, u32[]{:S(2)}) collective-permute-start(f32[4,32,1,128]{3,2,1,0:T(1,128)S(1)} %get-tuple-element.8), channel_id=1, source_target_pairs={{4,0},{8,4},{12,8},{16,12},{20,16},{24,20},{28,24},{32,28},{36,32}... | collective-permute-start | bytes 196616 | tf_op jit(solution)/shard_map/ppermute | solution.py:19
  176.7 4.4 %collective-permute-start.32 = (f32[4,1,16,128]{3,2,1,0:T(8,128)S(1)}, f32[4,1,16,128]{3,2,1,0:T(8,128)S(1)}, u32[]{:S(2)}, u32[]{:S(2)}) collective-permute-start(f32[4,1,16,128]{3,2,1,0:T(8,128)S(1)} %get-tuple-element.5), channel_id=1, source_target_pairs={{0,1},{1,2},{2,3},{4,5},{5,6},{6,7},{8,9},{9,10},{10,11},{12,13},{... | collective-permute-start | bytes 98312 | tf_op jit(solution)/shard_map/ppermute | solution.py:17
  179.2 5.2 %collective-permute-start.33 = (f32[4,1,16,128]{3,2,1,0:T(8,128)S(1)}, f32[4,1,16,128]{3,2,1,0:T(8,128)S(1)}, u32[]{:S(2)}, u32[]{:S(2)}) collective-permute-start(f32[4,1,16,128]{3,2,1,0:T(8,128)S(1)} %get-tuple-element.6), channel_id=1, source_target_pairs={{1,0},{2,1},{3,2},{5,4},{6,5},{7,6},{9,8},{10,9},{11,10},{13,12},{... | collective-permute-start | bytes 98312 | tf_op jit(solution)/shard_map/ppermute | solution.py:19
where the time goes:
time: 187 us; the launch traced here: 186 us
  starting transfers between devices  112 us (60%)
  matrix products  32.5 us (17%)
  waiting for transfers between devices  25 us (13%)
  other arithmetic  12.5 us (7%)
  local copies, waits for them, and re-layouts  4.03 us (2%)
    ppermute x18, starting transfers between devices, padded(): lax.ppermute(head, axis, [((i + 1) % count, i) for i in range(ends)])  84.5 us
    dot_general x2, matrix products, vertical_masked(): jnp.einsum(pattern, field, correlation, precision=lax.Precision.HIGHEST)  32.5 us
    ppermute x18, starting transfers between devices, padded(): lax.ppermute(tail, axis, [(i, (i + 1) % count) for i in range(ends)])  27.4 us
    ppermute x18, waiting for transfers between devices, padded(): lax.ppermute(head, axis, [((i + 1) % count, i) for i in range(ends)])  24.9 us
    add x6, other arithmetic, smooth(): centre + upper_face * (lat_padded[:, :-2] - centre)  8.79 us
  transfers between devices with their start and end apart: 36, of which 8 were waited for; matrix products, arithmetic and copies ran while one was open for 2% of the time, Pallas kernels for 0%

commit v1 on v0

v1 whole, which is shorter than its diff:
```python
import functools

import jax
import jax.numpy as jnp
from jax import lax
from jax.experimental import pallas as pl
from jax.experimental.pallas import tpu as pltpu
from jax.sharding import PartitionSpec as P

PASSES = 4
HALO = 4
MESH = pl.DeviceIdType.MESH
F32 = jnp.float32
BF16 = jnp.bfloat16

STEPS = ((-1, 0), (1, 0), (0, -1), (0, 1), (-1, -1), (1, -1), (-1, 1), (1, 1))
OPPOSITE = (1, 0, 3, 2, 7, 6, 5, 4)


def rolled(array, shift, axis):
    return pltpu.roll(array, shift % array.shape[axis], axis)


def lower_half(shape):
    return lax.broadcasted_iota(jnp.int32, shape, len(shape) - 2) < HALO


def pack_left(first, second):
    return jnp.where(lower_half(first.shape), first, rolled(second, HALO, 1))


def pack_right(first, second):
    return jnp.where(lower_half(first.shape), rolled(first, HALO, 1), second)


def unpack(from_right, from_left):
    low = lower_half(from_right.shape)
    first = jnp.where(low, from_right, rolled(from_left, HALO, 1))
    second = jnp.where(low, rolled(from_right, HALO, 1), from_left)
    return first, second


def halves(x):
    high = x.astype(BF16)
    return high, (x - high.astype(F32)).astype(BF16)


def kernel(
    lons, lats,
    ctl, obs, dev, wgt, dif, reg, cor, out,
    u1, u2, ct, ob, dv, corr, split, cx, cy, wb, regions, d_in, w_in, dt, dr,
    side_out, corner_out, side_in, corner_in,
    send_sem, recv_sem, dsend_sem, drecv_sem, small_sem, load_sem,
):
    variables, height, width, levels = ct.shape
    top, bottom = HALO, HALO + height
    me_lon, me_lat = lax.axis_index("lon"), lax.axis_index("lat")
    has_up, has_down = me_lat > 0, me_lat < lats - 1

    def neighbour(side):
        dlon, dlat = STEPS[side]
        return {"lon": lax.rem(me_lon + dlon + lons, lons), "lat": me_lat + dlat}

    def guarded(side, action):
        dlat = STEPS[side][1]
        if dlat == 0:
            action()
        else:
            pl.when(has_up if dlat < 0 else has_down)(action)

    barrier = pltpu.get_barrier_semaphore()
    for side in range(8):
        guarded(side, lambda side=side: pl.semaphore_signal(
            barrier, inc=1, device_id=neighbour(side), device_id_type=MESH))

    small = [
        pltpu.make_async_copy(dif, d_in, small_sem.at[0]),
        pltpu.make_async_copy(wgt, w_in, small_sem.at[1]),
        pltpu.make_async_copy(reg, regions, small_sem.at[2]),
    ]

    def own(ref, v):
        return ref.at[v, pl.ds(top, height), pl.ds(0, width)]

    def load(kind, v):
        source, target = (
            lambda: (ctl.at[v], own(u1, v)),
            lambda: (cor.at[:, v], corr.at[v]),
            lambda: (dev.at[v], dv.at[v]),
            lambda: (obs.at[v], ob.at[v]),
            lambda: (ctl.at[v], ct.at[v]),
        )[kind]()
        return pltpu.make_async_copy(source, target, load_sem.at[kind, v])

    for copy in small:
        copy.start()
    for kind in range(5):
        for v in range(variables):
            load(kind, v).start()

    def message(phase, v, side):
        if side < 2:
            source, target = side_out.at[phase, v, side], side_in.at[phase, v, OPPOSITE[side]]
        elif side < 4:
            row = 0 if side == 2 else height - HALO
            source = ctl.at[v, pl.ds(row, HALO)] if phase == 0 else u2.at[v, pl.ds(top + row, HALO), pl.ds(0, width)]
            row = bottom if side == 2 else 0
            target = (u1 if phase == 0 else u2).at[v, pl.ds(row, HALO), pl.ds(0, width)]
        else:
            source, target = corner_out.at[phase, v, side - 4], corner_in.at[phase, v, OPPOSITE[side] - 4]
        return pltpu.make_async_remote_copy(
            source, target, send_sem.at[phase, v, side], recv_sem.at[phase, v, OPPOSITE[side]],
            device_id=neighbour(side), device_id_type=MESH)

    def arrival(phase, v, side):
        if side < 2:
            target = side_in.at[phase, v, side]
        elif side < 4:
            target = (u1 if phase == 0 else u2).at[v, pl.ds(0 if side == 2 else bottom, HALO), pl.ds(0, width)]
        else:
            target = corner_in.at[phase, v, side - 4]
        return pltpu.make_async_remote_copy(
            target, target, send_sem.at[phase, v, side], recv_sem.at[phase, v, side],
            device_id=neighbour(side), device_id_type=MESH)

    def coefficients(side):
        dlon = STEPS[side][0]
        tile = pl.ds(0 if dlon <= 0 else 8, 8 if dlon else 16)
        return pltpu.make_async_remote_copy(
            dt.at[tile], dr.at[OPPOSITE[side], tile], dsend_sem.at[side], drecv_sem.at[OPPOSITE[side]],
            device_id=neighbour(side), device_id_type=MESH)

    def coefficients_in(side):
        dlon = STEPS[side][0]
        tile = pl.ds(0 if dlon >= 0 else 8, 8 if dlon else 16)
        return pltpu.make_async_remote_copy(
            dt.at[tile], dr.at[side, tile], dsend_sem.at[side], drecv_sem.at[side],
            device_id=neighbour(side), device_id_type=MESH)

    def pack(ref, phase, v):
        half = height // 2
        for side, columns, packer in ((0, pl.ds(0, 8), pack_left), (1, pl.ds(width - 8, 8), pack_right)):
            side_out[phase, v, side] = packer(
                ref[v, pl.ds(top, half), columns], ref[v, pl.ds(top + half, half), columns])
            corner_out[phase, v, side] = packer(
                ref[v, pl.ds(top, 2), columns], ref[v, pl.ds(top + 2, 2), columns])
            corner_out[phase, v, side + 2] = packer(
                ref[v, pl.ds(bottom - 4, 2), columns], ref[v, pl.ds(bottom - 2, 2), columns])

    def send(phase, v):
        for side in range(8):
            guarded(side, lambda side=side: message(phase, v, side).start())

    small[0].wait()
    small[1].wait()
    dt[...] = jnp.zeros_like(dt)
    dt[:, 0:height] = d_in[...]
    weight_t = w_in[...]

    load(0, 0).wait()
    pack(u1, 0, 0)

    pl.semaphore_wait(barrier, 2 + 3 * has_up.astype(jnp.int32) + 3 * has_down.astype(jnp.int32))

    for side in range(8):
        guarded(side, lambda side=side: coefficients(side).start())
    send(0, 0)

    @pl.loop(1, variables)
    def _(v):
        load(0, v).wait()
        pack(u1, 0, v)
        send(0, v)

    @pl.when(jnp.logical_not(has_up))
    def _():
        for ref in (u1, u2):
            ref[:, 0:top] = jnp.zeros((variables, HALO) + ref.shape[2:], F32)
        for side in (2, 4, 5):
            dr[side] = jnp.zeros(dr.shape[1:], F32)

    @pl.when(jnp.logical_not(has_down))
    def _():
        for ref in (u1, u2):
            ref[:, bottom:bottom + HALO] = jnp.zeros((variables, HALO) + ref.shape[2:], F32)
        for side in (3, 6, 7):
            dr[side] = jnp.zeros(dr.shape[1:], F32)

    for v in range(variables):
        load(1, v).wait()

        @pl.loop(0, corr.shape[1])
        def _(r):
            high, low = halves(corr[v, r])
            split[v, r, 0:levels] = high
            split[v, r, levels:2 * levels] = low

    for side in range(8):
        guarded(side, lambda side=side: coefficients_in(side).wait_recv())

    low = lower_half((8, 128))
    lane = lax.broadcasted_iota(jnp.int32, (24, 128), 1)

    def three(mid0, mid1, right, left):
        return jnp.concatenate([mid0, mid1, jnp.where(low, right, left)], axis=0)

    middle = three(dt[0:8], dt[8:16], dr[1, 0:8], dr[0, 8:16])
    above = three(dr[2, 0:8], dr[2, 8:16], dr[5, 0:8], dr[4, 8:16])
    below = three(dr[3, 0:8], dr[3, 8:16], dr[7, 0:8], dr[6, 8:16])
    grid = jnp.where(lane < top, rolled(above, HALO - height, 1), 0.0)
    grid = jnp.where((lane >= top) & (lane < bottom), rolled(middle, HALO, 1), grid)
    grid = jnp.where((lane >= bottom) & (lane < bottom + HALO), rolled(below, bottom, 1), grid)
    east = 0.5 * (grid + rolled(grid, -1, 0))
    south = 0.5 * (grid + rolled(grid, -1, 1))

    for r in range(height + 2 * HALO):
        cx[r] = jnp.broadcast_to(east[:, r:r + 1], (24, 128))
        cy[r] = jnp.broadcast_to(south[:, r:r + 1], (24, 128))
    for r in range(height):
        wb[r] = jnp.broadcast_to(weight_t[:, r:r + 1], (width, 128))

    keep_up = jnp.where(has_up, 1.0, 0.0).astype(F32)
    keep_down = jnp.where(has_down, 1.0, 0.0).astype(F32)

    def rows_step(ref, v, row, count, upper_flux, put, keep=None):
        here = ref[v, pl.ds(row, count)]
        after = ref[v, pl.ds(row + 1, count)]
        down = cy[pl.ds(row, count)] * (after - here)
        right = cx[pl.ds(row, count)] * (rolled(here, -1, 1) - here)
        up = upper_flux if count == 1 else jnp.concatenate([upper_flux, down[:-1]], axis=0)
        new = here + (down - up) + (right - rolled(right, 1, 1))
        if keep is not None:
            new = new * keep
        put(row, count, new)
        return down[count - 1:]

    def one_pass(ref, v, p, put):
        def store(row, count, new):
            ref[v, pl.ds(row, count)] = new

        flux = cy[p - 1:p] * (ref[v, p:p + 1] - ref[v, p - 1:p])
        if p < top:
            flux = rows_step(ref, v, p, top - p, flux, store, keep_up)

        def chunk(k, flux):
            return rows_step(ref, v, top + 4 * k, 4, flux, put or store)

        flux = lax.fori_loop(0, height // 4, chunk, flux)
        if p < top:
            rows_step(ref, v, bottom, top - p, flux, store, keep_down)

    def arrive(ref, phase, v):
        for side in range(8):
            guarded(side, lambda side=side: arrival(phase, v, side).wait_recv())
        columns = pl.ds(width, 8)
        half = height // 2
        first, second = unpack(side_in[phase, v, 1], side_in[phase, v, 0])
        ref[v, pl.ds(top, half), columns] = first
        ref[v, pl.ds(top + half, half), columns] = second

        @pl.when(has_up)
        def _():
            first, second = unpack(corner_in[phase, v, 1], corner_in[phase, v, 0])
            ref[v, pl.ds(0, 2), columns] = first
            ref[v, pl.ds(2, 2), columns] = second

        @pl.when(has_down)
        def _():
            first, second = unpack(corner_in[phase, v, 3], corner_in[phase, v, 2])
            ref[v, pl.ds(bottom, 2), columns] = first
            ref[v, pl.ds(bottom + 2, 2), columns] = second

    def joined(o):
        return o[:32, :levels] + (o[:32, levels:] + o[32:, :levels])

    small[2].wait()

    @pl.loop(0, variables)
    def _(v):
        arrive(u1, 0, v)
        for p in range(1, PASSES + 1):
            one_pass(u1, v, p, None)
        load(2, v).wait()
        load(3, v).wait()

        @pl.loop(0, height // 8)
        def _(pair):
            tiles = [(8 * pair + 4 * a, 8 * b) for a in range(2) for b in range(2)]

            def tile(ref, row, column):
                return ref[v, pl.ds(row, 4), pl.ds(column, 8)].reshape(32, levels)

            for row, column in tiles:
                matrix = split[v, regions[column, row]]
                lhs = jnp.concatenate(halves(tile(u1, top + row, column)), axis=0)
                state = joined(lax.dot_general(
                    lhs, matrix, (((1,), (1,)), ((), ())), preferred_element_type=F32))
                spread = tile(dv, row, column)
                weight = wb[pl.ds(row, 4), pl.ds(column, 8)].reshape(32, levels)
                weighted = spread * (weight * (spread * state - tile(ob, row, column)))
                lhs = jnp.concatenate(halves(weighted), axis=0)
                wide = jnp.concatenate([matrix[:levels], matrix[levels:]], axis=1)
                back = joined(jnp.dot(lhs, wide, preferred_element_type=F32))
                u2[v, pl.ds(top + row, 4), pl.ds(column, 8)] = back.reshape(4, 8, levels)

        pack(u2, 1, v)
        send(1, v)

    for v in range(variables):
        load(4, v).wait()

    @pl.loop(0, variables)
    def _(v):
        arrive(u2, 1, v)
        for side in (2, 3):
            guarded(side, lambda side=side: message(1, v, side).wait_send())
        for p in range(1, PASSES):
            one_pass(u2, v, p, None)

        def put(row, count, new):
            out[v, pl.ds(row - top, count)] = ct[v, pl.ds(row - top, count)] + new[:, :width]

        one_pass(u2, v, PASSES, put)

    @pl.loop(0, variables)
    def _(v):
        for phase in range(2):
            for side in range(8):
                if phase == 0 or side not in (2, 3):
                    guarded(side, lambda: message(phase, v, side).wait_send())

    for side in range(8):
        guarded(side, lambda side=side: coefficients(side).wait_send())


def on_device(lons, lats, control, observed, deviation, obs_weight, diffusivity, region_map, correlation):
    variables, height, width, levels = control.shape
    regions = correlation.shape[0]
    padded = (variables, height + 2 * HALO, width + 8, levels)
    anywhere = pl.BlockSpec(memory_space=pl.ANY)
    return pl.pallas_call(
        functools.partial(kernel, lons, lats),
        out_shape=jax.ShapeDtypeStruct(control.shape, F32),
        in_specs=[anywhere] * 7,
        out_specs=pl.BlockSpec(memory_space=pltpu.VMEM),
        scratch_shapes=[
            pltpu.VMEM(padded, F32),
            pltpu.VMEM(padded, F32),
            pltpu.VMEM(control.shape, F32),
            pltpu.VMEM(control.shape, F32),
            pltpu.VMEM(control.shape, F32),
            pltpu.VMEM((variables, regions, levels, levels), F32),
            pltpu.VMEM((variables, regions, 2 * levels, levels), BF16),
            pltpu.VMEM(padded[1:], F32),
            pltpu.VMEM(padded[1:], F32),
            pltpu.VMEM((height, width, levels), F32),
            pltpu.SMEM((width, height), jnp.int32),
            pltpu.VMEM((width, height), F32),
            pltpu.VMEM((width, height), F32),
            pltpu.VMEM((width, 128), F32),
            pltpu.VMEM((8, width, 128), F32),
            pltpu.VMEM((2, variables, 2, height // 2, 8, levels), F32),
            pltpu.VMEM((2, variables, 4, 2, 8, levels), F32),
            pltpu.VMEM((2, variables, 2, height // 2, 8, levels), F32),
            pltpu.VMEM((2, variables, 4, 2, 8, levels), F32),
            pltpu.SemaphoreType.DMA((2, variables, 8)),
            pltpu.SemaphoreType.DMA((2, variables, 8)),
            pltpu.SemaphoreType.DMA((8,)),
            pltpu.SemaphoreType.DMA((8,)),
            pltpu.SemaphoreType.DMA((3,)),
            pltpu.SemaphoreType.DMA((5, variables)),
        ],
        compiler_params=pltpu.CompilerParams(
            collective_id=0, has_side_effects=True, vmem_limit_bytes=60 * 2**20),
        cost_estimate=pl.CostEstimate(flops=10**9, bytes_accessed=8 * 2**20, transcendentals=0),
    )(control, observed, deviation, obs_weight.T, diffusivity.T, region_map.T, correlation)


def solution(mesh):
    field = P(None, "lat", "lon", None)
    cells = P("lat", "lon")
    return jax.shard_map(
        functools.partial(on_device, mesh.shape["lon"], mesh.shape["lat"]),
        mesh=mesh,
        in_specs=(field, field, field, cells, cells, cells, P()),
        out_specs=field,
        check_vma=False,
    )
```

time: 187 us -> 48.2 us (0.26)
  starting transfers between devices: 112 us -> 0 us
  Pallas kernels: 0 us -> 45.8 us
  matrix products: 32.5 us -> 0 us
  waiting for transfers between devices: 25 us -> 0 us
  other arithmetic: 12.5 us -> 0 us
    ppermute x36 -> x0, starting transfers between devices: 112 us -> none  [the longest x18 84.5 us: padded(): lax.ppermute(head, axis, [((i + 1) % count, i) for i in range(ends)])]
    pallas_call x0 -> x1, Pallas kernels: none -> 45.8 us  [on_device(): pl.pallas_call(functools.partial(kernel, lons, lats), out_shape=jax.Shape...]
    dot_general x2 -> x0, matrix products: 32.5 us -> none  [vertical_masked(): jnp.einsum(pattern, field, correlation, precision=lax.Precision.HIGHEST)]
    ppermute x36 -> x0, waiting for transfers between devices: 25 us -> none  [the longest x18 24.9 us: padded(): lax.ppermute(head, axis, [((i + 1) % count, i) for i in range(ends)])]
    add x7 -> x0, other arithmetic: 10.8 us -> none  [the longest x6 8.79 us: smooth(): centre + upper_face * (lat_padded[:, :-2] - centre)]
    slice x18 -> x0, local copies, waits for them, and re-layouts: 3.56 us -> none  [padded(): lax.slice_in_dim(cells, cells.shape[dim] - width, cells.shape[dim], axis=...]
    unnamed x14 -> x1, local copies, waits for them, and re-layouts: 0.17 us -> 2.29 us
  transfers between devices with their start and end apart: 36 -> 0, of which waited for: 8 -> 0; matrix products, arithmetic and copies ran while one was open for 2% -> 0% of each run, Pallas kernels for 0% -> 0%
where the time goes in v1:
time: 48.2 us; the launch traced here: 48.1 us
  Pallas kernels  45.8 us (95%)
  local copies, waits for them, and re-layouts  2.29 us (5%)
    pallas_call x1, Pallas kernels, on_device(): pl.pallas_call(functools.partial(kernel, lons, lats), out_shape=jax.Shape...  45.8 us
    unnamed x1, local copies, waits for them, and re-layouts  2.29 us

profile of v1, /device:TPU:1, one launch (start us, length us, event | category | flops | bytes accessed | tf_op | source)
XLA Modules:
  0.0 48.1 jit_solution(8103950682186176964)
XLA Ops:
  0.0 45.8 %shard_map.73 = f32[4,32,16,128]{3,2,1,0:T(8,128)} custom-call(f32[4,32,16,128]{3,2,1,0:T(8,128)} %ctl.1, f32[4,32,16,128]{3,2,1,0:T(8,128)} %obs.1, f32[4,32,16,128]{3,2,1,0:T(8,128)} %dev.1, f32[16,32]{1,0:T(8,128)} %bitcast.3, f32[16,32]{1,0:T(8,128)} %bitcast.4, s32[16,32]{1,0:T(8,128)} %bitcast.5, f32[16,4,128,128]{3,2,1,0:T(8,128)} %cor.1), custom_call_target="tpu_custom_call" | custom-call | flops 1000000000 | bytes 8388608 | tf_op jit(solution)/shard_map/pallas_call | solution.py:341
  45.8 2.3 %copy.9 = f32[4,32,16,128]{3,2,1,0:T(8,128)} copy(f32[4,32,16,128]{3,2,1,0:T(8,128)} %shard_map.73) | data formatting | bytes 2097152

commit v2 on v1

--- a/solution.py
+++ b/solution.py
@@ -9,6 +9,8 @@
 
 PASSES = 4
 HALO = 4
+CHUNK = 8
+GROUP = 4
 MESH = pl.DeviceIdType.MESH
 F32 = jnp.float32
 BF16 = jnp.bfloat16
@@ -33,11 +35,14 @@
     return jnp.where(lower_half(first.shape), rolled(first, HALO, 1), second)
 
 
-def unpack(from_right, from_left):
-    low = lower_half(from_right.shape)
-    first = jnp.where(low, from_right, rolled(from_left, HALO, 1))
-    second = jnp.where(low, rolled(from_right, HALO, 1), from_left)
-    return first, second
+def corner_left(near, middle, far):
+    place = lax.broadcasted_iota(jnp.int32, near.shape, 1)
+    return jnp.where(place < 3, near, jnp.where(place < 5, rolled(middle, 3, 1), rolled(far, 5, 1)))
+
+
+def corner_right(near, middle, far):
+    place = lax.broadcasted_iota(jnp.int32, near.shape, 1)
+    return jnp.where(place > 4, near, jnp.where(place > 2, rolled(middle, -3, 1), rolled(far, -5, 1)))
 
 
 def halves(x):
@@ -48,12 +53,13 @@
 def kernel(
     lons, lats,
     ctl, obs, dev, wgt, dif, reg, cor, out,
-    u1, u2, ct, ob, dv, corr, split, cx, cy, wb, regions, d_in, w_in, dt, dr,
+    u1, u2, ct, ob, dv, corr, split, c0, cx, cy, wb, regions, d_in, w_in, dt, dr,
     side_out, corner_out, side_in, corner_in,
     send_sem, recv_sem, dsend_sem, drecv_sem, small_sem, load_sem,
 ):
     variables, height, width, levels = ct.shape
     top, bottom = HALO, HALO + height
+    left, right = 8, 8 + width
     me_lon, me_lat = lax.axis_index("lon"), lax.axis_index("lat")
     has_up, has_down = me_lat > 0, me_lat < lats - 1
 
@@ -80,7 +86,7 @@
     ]
 
     def own(ref, v):
-        return ref.at[v, pl.ds(top, height), pl.ds(0, width)]
+        return ref.at[v, pl.ds(top, height), pl.ds(left, width)]
 
     def load(kind, v):
         source, target = (
@@ -103,9 +109,9 @@
             source, target = side_out.at[phase, v, side], side_in.at[phase, v, OPPOSITE[side]]
         elif side < 4:
             row = 0 if side == 2 else height - HALO
-            source = ctl.at[v, pl.ds(row, HALO)] if phase == 0 else u2.at[v, pl.ds(top + row, HALO), pl.ds(0, width)]
+            source = ctl.at[v, pl.ds(row, HALO)] if phase == 0 else u2.at[v, pl.ds(top + row, HALO), pl.ds(left, width)]
             row = bottom if side == 2 else 0
-            target = (u1 if phase == 0 else u2).at[v, pl.ds(row, HALO), pl.ds(0, width)]
+            target = (u1 if phase == 0 else u2).at[v, pl.ds(row, HALO), pl.ds(left, width)]
         else:
             source, target = corner_out.at[phase, v, side - 4], corner_in.at[phase, v, OPPOSITE[side] - 4]
         return pltpu.make_async_remote_copy(
@@ -116,7 +122,7 @@
         if side < 2:
             target = side_in.at[phase, v, side]
         elif side < 4:
-            target = (u1 if phase == 0 else u2).at[v, pl.ds(0 if side == 2 else bottom, HALO), pl.ds(0, width)]
+            target = (u1 if phase == 0 else u2).at[v, pl.ds(0 if side == 2 else bottom, HALO), pl.ds(left, width)]
         else:
             target = corner_in.at[phase, v, side - 4]
         return pltpu.make_async_remote_copy(
@@ -139,13 +145,12 @@
 
     def pack(ref, phase, v):
         half = height // 2
-        for side, columns, packer in ((0, pl.ds(0, 8), pack_left), (1, pl.ds(width - 8, 8), pack_right)):
+        for side, column, packer, corner in ((0, left, pack_left, corner_left), (1, right - 8, pack_right, corner_right)):
+            columns = pl.ds(column, 8)
             side_out[phase, v, side] = packer(
                 ref[v, pl.ds(top, half), columns], ref[v, pl.ds(top + half, half), columns])
-            corner_out[phase, v, side] = packer(
-                ref[v, pl.ds(top, 2), columns], ref[v, pl.ds(top + 2, 2), columns])
-            corner_out[phase, v, side + 2] = packer(
-                ref[v, pl.ds(bottom - 4, 2), columns], ref[v, pl.ds(bottom - 2, 2), columns])
+            for place, rows in ((side, (top, top + 1, top + 2)), (side + 2, (bottom - 1, bottom - 2, bottom - 3))):
+                corner_out[phase, v, place] = corner(*(ref[v, pl.ds(row, 1), columns] for row in rows))[0]
 
     def send(phase, v):
         for side in range(8):
@@ -198,77 +203,83 @@
     for side in range(8):
         guarded(side, lambda side=side: coefficients_in(side).wait_recv())
 
-    low = lower_half((8, 128))
-    lane = lax.broadcasted_iota(jnp.int32, (24, 128), 1)
-
-    def three(mid0, mid1, right, left):
-        return jnp.concatenate([mid0, mid1, jnp.where(low, right, left)], axis=0)
-
-    middle = three(dt[0:8], dt[8:16], dr[1, 0:8], dr[0, 8:16])
-    above = three(dr[2, 0:8], dr[2, 8:16], dr[5, 0:8], dr[4, 8:16])
-    below = three(dr[3, 0:8], dr[3, 8:16], dr[7, 0:8], dr[6, 8:16])
+    lane = lax.broadcasted_iota(jnp.int32, (width + 16, 128), 1)
+
+    def across(own, from_left, from_right):
+        return jnp.concatenate([from_left[8:16], own[0:16], from_right[0:8]], axis=0)
+
+    middle = across(dt, dr[0], dr[1])
+    above = across(dr[2], dr[4], dr[5])
+    below = across(dr[3], dr[6], dr[7])
     grid = jnp.where(lane < top, rolled(above, HALO - height, 1), 0.0)
     grid = jnp.where((lane >= top) & (lane < bottom), rolled(middle, HALO, 1), grid)
     grid = jnp.where((lane >= bottom) & (lane < bottom + HALO), rolled(below, bottom, 1), grid)
     east = 0.5 * (grid + rolled(grid, -1, 0))
     south = 0.5 * (grid + rolled(grid, -1, 1))
+    rest = 1.0 - (east + rolled(east, 1, 0)) - (south + rolled(south, 1, 1))
+    first_row = jnp.where(has_up, 0, top)
+    last_row = jnp.where(has_down, bottom + HALO, bottom)
+    inside = (lane >= first_row) & (lane < last_row)
+    rest = jnp.where(inside, rest, 0.0)
+    east = jnp.where(inside, east, 0.0)
+    south = jnp.where(inside & (lane < last_row - 1), south, 0.0)
 
     for r in range(height + 2 * HALO):
-        cx[r] = jnp.broadcast_to(east[:, r:r + 1], (24, 128))
-        cy[r] = jnp.broadcast_to(south[:, r:r + 1], (24, 128))
+        for coefficient, ref in ((rest, c0), (east, cx), (south, cy)):
+            ref[r] = jnp.broadcast_to(coefficient[:, r:r + 1], ref.shape[1:])
     for r in range(height):
         wb[r] = jnp.broadcast_to(weight_t[:, r:r + 1], (width, 128))
 
-    keep_up = jnp.where(has_up, 1.0, 0.0).astype(F32)
-    keep_down = jnp.where(has_down, 1.0, 0.0).astype(F32)
-
-    def rows_step(ref, v, row, count, upper_flux, put, keep=None):
-        here = ref[v, pl.ds(row, count)]
-        after = ref[v, pl.ds(row + 1, count)]
-        down = cy[pl.ds(row, count)] * (after - here)
-        right = cx[pl.ds(row, count)] * (rolled(here, -1, 1) - here)
-        up = upper_flux if count == 1 else jnp.concatenate([upper_flux, down[:-1]], axis=0)
-        new = here + (down - up) + (right - rolled(right, 1, 1))
-        if keep is not None:
-            new = new * keep
+    def rows_step(ref, v, row, count, above, first, last, put):
+        here_columns = pl.ds(first, last - first)
+        block = ref[v, pl.ds(row, count + 1), here_columns]
+        here = block[:count]
+        up = above if count == 1 else jnp.concatenate([above, here[:-1]], axis=0)
+        rows = pl.ds(row, count)
+        faces = cy[pl.ds(row - 1, count + 1), here_columns]
+        new = c0[rows, here_columns] * here + (faces[1:] * block[1:] + faces[:-1] * up)
+        new = new + (cx[rows, here_columns] * ref[v, rows, pl.ds(first + 1, last - first)]
+                     + cx[rows, pl.ds(first - 1, last - first)] * ref[v, rows, pl.ds(first - 1, last - first)])
         put(row, count, new)
-        return down[count - 1:]
+        return here[count - 1:]
 
     def one_pass(ref, v, p, put):
+        first, last = (left - HALO, right + HALO) if p < PASSES else (left, right)
+        here_columns = pl.ds(first, last - first)
+
         def store(row, count, new):
-            ref[v, pl.ds(row, count)] = new
-
-        flux = cy[p - 1:p] * (ref[v, p:p + 1] - ref[v, p - 1:p])
-        if p < top:
-            flux = rows_step(ref, v, p, top - p, flux, store, keep_up)
-
-        def chunk(k, flux):
-            return rows_step(ref, v, top + 4 * k, 4, flux, put or store)
-
-        flux = lax.fori_loop(0, height // 4, chunk, flux)
-        if p < top:
-            rows_step(ref, v, bottom, top - p, flux, store, keep_down)
+            ref[v, pl.ds(row, count), here_columns] = new
+
+        above = ref[v, p - 1:p, here_columns]
+        if p < PASSES:
+            above = rows_step(ref, v, p, top - p, above, first, last, store)
+
+        def chunk(k, above):
+            return rows_step(ref, v, top + CHUNK * k, CHUNK, above, first, last, put or store)
+
+        above = lax.fori_loop(0, height // CHUNK, chunk, above)
+        if p < PASSES:
+            rows_step(ref, v, bottom, top - p, above, first, last, store)
 
     def arrive(ref, phase, v):
         for side in range(8):
             guarded(side, lambda side=side: arrival(phase, v, side).wait_recv())
-        columns = pl.ds(width, 8)
         half = height // 2
-        first, second = unpack(side_in[phase, v, 1], side_in[phase, v, 0])
-        ref[v, pl.ds(top, half), columns] = first
-        ref[v, pl.ds(top + half, half), columns] = second
-
-        @pl.when(has_up)
-        def _():
-            first, second = unpack(corner_in[phase, v, 1], corner_in[phase, v, 0])
-            ref[v, pl.ds(0, 2), columns] = first
-            ref[v, pl.ds(2, 2), columns] = second
-
-        @pl.when(has_down)
-        def _():
-            first, second = unpack(corner_in[phase, v, 3], corner_in[phase, v, 2])
-            ref[v, pl.ds(bottom, 2), columns] = first
-            ref[v, pl.ds(bottom + 2, 2), columns] = second
+        to_left, to_right = pl.ds(left - 8, 8), pl.ds(right, 8)
+        from_left, from_right = side_in[phase, v, 0], side_in[phase, v, 1]
+        ref[v, pl.ds(top, half), to_left] = rolled(from_left, HALO, 1)
+        ref[v, pl.ds(top + half, half), to_left] = from_left
+        ref[v, pl.ds(top, half), to_right] = from_right
+        ref[v, pl.ds(top + half, half), to_right] = rolled(from_right, HALO, 1)
+
+        def corners(place, rows):
+            for n, row in enumerate(rows):
+                turn = (0, 3, 5)[n]
+                ref[v, row, to_left] = rolled(corner_in[phase, v, place], turn, 0)
+                ref[v, row, to_right] = rolled(corner_in[phase, v, place + 1], -turn, 0)
+
+        pl.when(has_up)(lambda: corners(0, (top - 1, top - 2, top - 3)))
+        pl.when(has_down)(lambda: corners(2, (bottom, bottom + 1, bottom + 2)))
 
     def joined(o):
         return o[:32, :levels] + (o[:32, levels:] + o[32:, :levels])
@@ -283,25 +294,37 @@
         load(2, v).wait()
         load(3, v).wait()
 
-        @pl.loop(0, height // 8)
-        def _(pair):
-            tiles = [(8 * pair + 4 * a, 8 * b) for a in range(2) for b in range(2)]
-
-            def tile(ref, row, column):
-                return ref[v, pl.ds(row, 4), pl.ds(column, 8)].reshape(32, levels)
-
-            for row, column in tiles:
-                matrix = split[v, regions[column, row]]
-                lhs = jnp.concatenate(halves(tile(u1, top + row, column)), axis=0)
-                state = joined(lax.dot_general(
-                    lhs, matrix, (((1,), (1,)), ((), ())), preferred_element_type=F32))
-                spread = tile(dv, row, column)
-                weight = wb[pl.ds(row, 4), pl.ds(column, 8)].reshape(32, levels)
-                weighted = spread * (weight * (spread * state - tile(ob, row, column)))
-                lhs = jnp.concatenate(halves(weighted), axis=0)
-                wide = jnp.concatenate([matrix[:levels], matrix[levels:]], axis=1)
-                back = joined(jnp.dot(lhs, wide, preferred_element_type=F32))
-                u2[v, pl.ds(top + row, 4), pl.ds(column, 8)] = back.reshape(4, 8, levels)
+        def tile(ref, row, column):
+            return ref[v, pl.ds(row, 4), pl.ds(column, 8)].reshape(32, levels)
+
+        def forward(row, column):
+            matrix = split[v, regions[column, row]]
+            lhs = jnp.concatenate(halves(tile(u1, top + row, left + column)), axis=0)
+            return lax.dot_general(lhs, matrix, (((1,), (1,)), ((), ())), preferred_element_type=F32)
+
+        def adjoint(row, column, product):
+            matrix = split[v, regions[column, row]]
+            spread = tile(dv, row, column)
+            weight = wb[pl.ds(row, 4), pl.ds(column, 8)].reshape(32, levels)
+            weighted = spread * (weight * (spread * joined(product) - tile(ob, row, column)))
+            lhs = jnp.concatenate(halves(weighted), axis=0)
+            wide = jnp.concatenate([matrix[:levels], matrix[levels:]], axis=1)
+            return jnp.dot(lhs, wide, preferred_element_type=F32)
+
+        def finish(row, column, product):
+            u2[v, pl.ds(top + row, 4), pl.ds(left + column, 8)] = joined(product).reshape(4, 8, levels)
+
+        tiles = [(4 * a, 8 * b) for a in range(height // 4) for b in range(width // 8)]
+        groups = [tiles[n:n + GROUP] for n in range(0, len(tiles), GROUP)]
+        forwards, adjoints = {}, {}
+        for n in range(len(groups) + 2):
+            if n < len(groups):
+                forwards[n] = [forward(*t) for t in groups[n]]
+            if 0 <= n - 1 < len(groups):
+                adjoints[n - 1] = [adjoint(*t, o) for t, o in zip(groups[n - 1], forwards.pop(n - 1))]
+            if n >= 2:
+                for t, o in zip(groups[n - 2], adjoints.pop(n - 2)):
+                    finish(*t, o)
 
         pack(u2, 1, v)
         send(1, v)
@@ -318,7 +341,7 @@
             one_pass(u2, v, p, None)
 
         def put(row, count, new):
-            out[v, pl.ds(row - top, count)] = ct[v, pl.ds(row - top, count)] + new[:, :width]
+            out[v, pl.ds(row - top, count)] = ct[v, pl.ds(row - top, count)] + new
 
         one_pass(u2, v, PASSES, put)
 
@@ -336,12 +359,12 @@
 def on_device(lons, lats, control, observed, deviation, obs_weight, diffusivity, region_map, correlation):
     variables, height, width, levels = control.shape
     regions = correlation.shape[0]
-    padded = (variables, height + 2 * HALO, width + 8, levels)
-    anywhere = pl.BlockSpec(memory_space=pl.ANY)
+    padded = (variables, height + 2 * HALO, width + 16, levels)
+    in_hbm = pl.BlockSpec(memory_space=pltpu.HBM)
     return pl.pallas_call(
         functools.partial(kernel, lons, lats),
         out_shape=jax.ShapeDtypeStruct(control.shape, F32),
-        in_specs=[anywhere] * 7,
+        in_specs=[in_hbm] * 7,
         out_specs=pl.BlockSpec(memory_space=pltpu.VMEM),
         scratch_shapes=[
             pltpu.VMEM(padded, F32),
@@ -353,6 +376,7 @@
             pltpu.VMEM((variables, regions, 2 * levels, levels), BF16),
             pltpu.VMEM(padded[1:], F32),
             pltpu.VMEM(padded[1:], F32),
+            pltpu.VMEM(padded[1:], F32),
             pltpu.VMEM((height, width, levels), F32),
             pltpu.SMEM((width, height), jnp.int32),
             pltpu.VMEM((width, height), F32),
@@ -360,9 +384,9 @@
             pltpu.VMEM((width, 128), F32),
             pltpu.VMEM((8, width, 128), F32),
             pltpu.VMEM((2, variables, 2, height // 2, 8, levels), F32),
-            pltpu.VMEM((2, variables, 4, 2, 8, levels), F32),
+            pltpu.VMEM((2, variables, 4, 8, levels), F32),
             pltpu.VMEM((2, variables, 2, height // 2, 8, levels), F32),
-            pltpu.VMEM((2, variables, 4, 2, 8, levels), F32),
+            pltpu.VMEM((2, variables, 4, 8, levels), F32),
             pltpu.SemaphoreType.DMA((2, variables, 8)),
             pltpu.SemaphoreType.DMA((2, variables, 8)),
             pltpu.SemaphoreType.DMA((8,)),
@@ -371,7 +395,7 @@
             pltpu.SemaphoreType.DMA((5, variables)),
         ],
         compiler_params=pltpu.CompilerParams(
-            collective_id=0, has_side_effects=True, vmem_limit_bytes=60 * 2**20),
+            collective_id=0, has_side_effects=True, vmem_limit_bytes=52 * 2**20),
         cost_estimate=pl.CostEstimate(flops=10**9, bytes_accessed=8 * 2**20, transcendentals=0),
     )(control, observed, deviation, obs_weight.T, diffusivity.T, region_map.T, correlation)
 

time: 48.2 us -> 36.8 us (0.76)
  Pallas kernels: 45.8 us -> 33.5 us
  local copies, waits for them, and re-layouts: 2.29 us -> 3.06 us
    pallas_call x1, Pallas kernels: 45.8 us -> 33.5 us  [on_device(): pl.pallas_call(functools.partial(kernel, lons, lats), out_shape=jax.Shape...]
    unnamed x1 -> x7, local copies, waits for them, and re-layouts: 2.29 us -> 3.06 us
where the time goes in v2:
time: 36.8 us; the launch traced here: 36.6 us
  Pallas kernels  33.5 us (91%)
  local copies, waits for them, and re-layouts  3.06 us (8%)
    pallas_call x1, Pallas kernels, on_device(): pl.pallas_call(functools.partial(kernel, lons, lats), out_shape=jax.Shape...  33.5 us
    unnamed x7, local copies, waits for them, and re-layouts  3.06 us

profile of v2, /device:TPU:1, one launch (start us, length us, event | category | flops | bytes accessed | tf_op | source)
XLA Modules:
  0.0 36.6 jit_solution(3078258514245366362)
XLA Ops:
  0.0 0.0 copy-start
  0.0 0.7 %copy-done = f32[32,16]{0,1:T(8,128)S(1)} copy-done((f32[32,16]{0,1:T(8,128)S(1)}, f32[32,16]{0,1:T(8,128)}, u32[]{:S(2)}) %copy-start) | copy-done | bytes 2072
  0.7 0.0 copy-start.1
  0.7 0.7 %copy-done.1 = f32[32,16]{0,1:T(8,128)S(1)} copy-done((f32[32,16]{0,1:T(8,128)S(1)}, f32[32,16]{0,1:T(8,128)}, u32[]{:S(2)}) %copy-start.1) | copy-done | bytes 2072
  1.4 0.0 copy-start.2
  1.4 0.7 %copy-done.2 = s32[32,16]{0,1:T(8,128)S(1)} copy-done((s32[32,16]{0,1:T(8,128)S(1)}, s32[32,16]{0,1:T(8,128)}, u32[]{:S(2)}) %copy-start.2) | copy-done | bytes 2072
  2.1 33.5 %shard_map.73 = f32[4,32,16,128]{3,2,1,0:T(8,128)S(1)} custom-call(f32[4,32,16,128]{3,2,1,0:T(8,128)} %ctl.1, f32[4,32,16,128]{3,2,1,0:T(8,128)} %obs.1, f32[4,32,16,128]{3,2,1,0:T(8,128)} %dev.1, f32[16,32]{1,0:T(8,128)S(1)} %bitcast.3, f32[16,32]{1,0:T(8,128)S(1)} %bitcast.4, s32[16,32]{1,0:T(8,128)S(1)} %bitcast.5, f32[16,4,128,128]{3,2,1,0:T(8,128)} %cor.1), custom_call_target="tpu_custom_call" | custom-call | flops 1000000000 | bytes 8388608 | tf_op jit(solution)/shard_map/pallas_call | solution.py:364
  35.6 1.0 %copy.9 = f32[4,32,16,128]{3,2,1,0:T(8,128)} copy(f32[4,32,16,128]{3,2,1,0:T(8,128)S(1)} %shard_map.73) | data formatting | bytes 2097152
Async XLA Ops:
  0.0 0.7 %copy-start = (f32[32,16]{0,1:T(8,128)S(1)}, f32[32,16]{0,1:T(8,128)}, u32[]{:S(2)}) copy-start(f32[32,16]{0,1:T(8,128)} %param.10) | copy-start | bytes 6148
  0.7 0.7 %copy-start.1 = (f32[32,16]{0,1:T(8,128)S(1)}, f32[32,16]{0,1:T(8,128)}, u32[]{:S(2)}) copy-start(f32[32,16]{0,1:T(8,128)} %param.11) | copy-start | bytes 6148
  1.4 0.7 %copy-start.2 = (s32[32,16]{0,1:T(8,128)S(1)}, s32[32,16]{0,1:T(8,128)}, u32[]{:S(2)}) copy-start(s32[32,16]{0,1:T(8,128)} %param.12) | copy-start | bytes 6148

commit v3 on v2

--- a/solution.py
+++ b/solution.py
@@ -9,8 +9,8 @@
 
 PASSES = 4
 HALO = 4
-CHUNK = 8
-GROUP = 4
+CHUNK = 16
+GROUP = 8
 MESH = pl.DeviceIdType.MESH
 F32 = jnp.float32
 BF16 = jnp.bfloat16
@@ -52,8 +52,8 @@
 
 def kernel(
     lons, lats,
-    ctl, obs, dev, wgt, dif, reg, cor, out,
-    u1, u2, ct, ob, dv, corr, split, c0, cx, cy, wb, regions, d_in, w_in, dt, dr,
+    ctl, obs, dev, pair, reg, cor, out,
+    u1, u2, ct, ob, dv, corr, split, c0, cx, cw, cy, wb, regions, dt, dr,
     side_out, corner_out, side_in, corner_in,
     send_sem, recv_sem, dsend_sem, drecv_sem, small_sem, load_sem,
 ):
@@ -79,11 +79,7 @@
         guarded(side, lambda side=side: pl.semaphore_signal(
             barrier, inc=1, device_id=neighbour(side), device_id_type=MESH))
 
-    small = [
-        pltpu.make_async_copy(dif, d_in, small_sem.at[0]),
-        pltpu.make_async_copy(wgt, w_in, small_sem.at[1]),
-        pltpu.make_async_copy(reg, regions, small_sem.at[2]),
-    ]
+    region_copy = pltpu.make_async_copy(reg, regions, small_sem.at[0])
 
     def own(ref, v):
         return ref.at[v, pl.ds(top, height), pl.ds(left, width)]
@@ -98,11 +94,10 @@
         )[kind]()
         return pltpu.make_async_copy(source, target, load_sem.at[kind, v])
 
-    for copy in small:
-        copy.start()
-    for kind in range(5):
+    for kind in range(4):
         for v in range(variables):
             load(kind, v).start()
+    region_copy.start()
 
     def message(phase, v, side):
         if side < 2:
@@ -153,14 +148,12 @@
                 corner_out[phase, v, place] = corner(*(ref[v, pl.ds(row, 1), columns] for row in rows))[0]
 
     def send(phase, v):
-        for side in range(8):
+        for side in (4, 5, 6, 7, 2, 3, 0, 1):
             guarded(side, lambda side=side: message(phase, v, side).start())
 
-    small[0].wait()
-    small[1].wait()
     dt[...] = jnp.zeros_like(dt)
-    dt[:, 0:height] = d_in[...]
-    weight_t = w_in[...]
+    dt[:, 0:height] = pair[0:width]
+    weight_t = pair[width:2 * width]
 
     load(0, 0).wait()
     pack(u1, 0, 0)
@@ -224,22 +217,28 @@
     east = jnp.where(inside, east, 0.0)
     south = jnp.where(inside & (lane < last_row - 1), south, 0.0)
 
+    kept = width + 2 * HALO
+    start = left - HALO
+    west = rolled(east, 1 - start, 0)[:kept]
+    rest, east, south = (rolled(x, -start, 0)[:kept] for x in (rest, east, south))
+
     for r in range(height + 2 * HALO):
-        for coefficient, ref in ((rest, c0), (east, cx), (south, cy)):
+        for coefficient, ref in ((rest, c0), (east, cx), (west, cw), (south, cy)):
             ref[r] = jnp.broadcast_to(coefficient[:, r:r + 1], ref.shape[1:])
     for r in range(height):
         wb[r] = jnp.broadcast_to(weight_t[:, r:r + 1], (width, 128))
 
     def rows_step(ref, v, row, count, above, first, last, put):
         here_columns = pl.ds(first, last - first)
+        kept_columns = pl.ds(first - start, last - first)
         block = ref[v, pl.ds(row, count + 1), here_columns]
         here = block[:count]
         up = above if count == 1 else jnp.concatenate([above, here[:-1]], axis=0)
         rows = pl.ds(row, count)
-        faces = cy[pl.ds(row - 1, count + 1), here_columns]
-        new = c0[rows, here_columns] * here + (faces[1:] * block[1:] + faces[:-1] * up)
-        new = new + (cx[rows, here_columns] * ref[v, rows, pl.ds(first + 1, last - first)]
-                     + cx[rows, pl.ds(first - 1, last - first)] * ref[v, rows, pl.ds(first - 1, last - first)])
+        faces = cy[pl.ds(row - 1, count + 1), kept_columns]
+        new = c0[rows, kept_columns] * here + (faces[1:] * block[1:] + faces[:-1] * up)
+        new = new + (cx[rows, kept_columns] * ref[v, rows, pl.ds(first + 1, last - first)]
+                     + cw[rows, kept_columns] * ref[v, rows, pl.ds(first - 1, last - first)])
         put(row, count, new)
         return here[count - 1:]
 
@@ -284,7 +283,9 @@
     def joined(o):
         return o[:32, :levels] + (o[:32, levels:] + o[32:, :levels])
 
-    small[2].wait()
+    region_copy.wait()
+    for v in range(variables):
+        load(4, v).start()
 
     @pl.loop(0, variables)
     def _(v):
@@ -329,11 +330,9 @@
         pack(u2, 1, v)
         send(1, v)
 
-    for v in range(variables):
-        load(4, v).wait()
-
     @pl.loop(0, variables)
     def _(v):
+        load(4, v).wait()
         arrive(u2, 1, v)
         for side in (2, 3):
             guarded(side, lambda side=side: message(1, v, side).wait_send())
@@ -360,11 +359,12 @@
     variables, height, width, levels = control.shape
     regions = correlation.shape[0]
     padded = (variables, height + 2 * HALO, width + 16, levels)
+    pair = jnp.concatenate([diffusivity.T, obs_weight.T], axis=0)
     in_hbm = pl.BlockSpec(memory_space=pltpu.HBM)
     return pl.pallas_call(
         functools.partial(kernel, lons, lats),
         out_shape=jax.ShapeDtypeStruct(control.shape, F32),
-        in_specs=[in_hbm] * 7,
+        in_specs=[in_hbm] * 3 + [pl.BlockSpec(memory_space=pltpu.VMEM)] + [in_hbm] * 2,
         out_specs=pl.BlockSpec(memory_space=pltpu.VMEM),
         scratch_shapes=[
             pltpu.VMEM(padded, F32),
@@ -374,13 +374,12 @@
             pltpu.VMEM(control.shape, F32),
             pltpu.VMEM((variables, regions, levels, levels), F32),
             pltpu.VMEM((variables, regions, 2 * levels, levels), BF16),
-            pltpu.VMEM(padded[1:], F32),
-            pltpu.VMEM(padded[1:], F32),
-            pltpu.VMEM(padded[1:], F32),
+            pltpu.VMEM((height + 2 * HALO, width + 2 * HALO, levels), F32),
+            pltpu.VMEM((height + 2 * HALO, width + 2 * HALO, levels), F32),
+            pltpu.VMEM((height + 2 * HALO, width + 2 * HALO, levels), F32),
+            pltpu.VMEM((height + 2 * HALO, width + 2 * HALO, levels), F32),
             pltpu.VMEM((height, width, levels), F32),
             pltpu.SMEM((width, height), jnp.int32),
-            pltpu.VMEM((width, height), F32),
-            pltpu.VMEM((width, height), F32),
             pltpu.VMEM((width, 128), F32),
             pltpu.VMEM((8, width, 128), F32),
             pltpu.VMEM((2, variables, 2, height // 2, 8, levels), F32),
@@ -391,13 +390,13 @@
             pltpu.SemaphoreType.DMA((2, variables, 8)),
             pltpu.SemaphoreType.DMA((8,)),
             pltpu.SemaphoreType.DMA((8,)),
-            pltpu.SemaphoreType.DMA((3,)),
+            pltpu.SemaphoreType.DMA((1,)),
             pltpu.SemaphoreType.DMA((5, variables)),
         ],
         compiler_params=pltpu.CompilerParams(
             collective_id=0, has_side_effects=True, vmem_limit_bytes=52 * 2**20),
         cost_estimate=pl.CostEstimate(flops=10**9, bytes_accessed=8 * 2**20, transcendentals=0),
-    )(control, observed, deviation, obs_weight.T, diffusivity.T, region_map.T, correlation)
+    )(control, observed, deviation, pair, region_map.T, correlation)
 
 
 def solution(mesh):

time: 36.8 us -> 35.3 us (0.959)
  local copies, waits for them, and re-layouts: 3.06 us -> 1.67 us
  Pallas kernels: 33.5 us -> 32.6 us
  other arithmetic: 0 us -> 0.72 us
    unnamed x7 -> x3, local copies, waits for them, and re-layouts: 3.06 us -> 1.67 us
    pallas_call x1, Pallas kernels: 33.5 us -> 32.6 us  [on_device(): pl.pallas_call(functools.partial(kernel, lons, lats), out_shape=jax.Shape...]
    concatenate x0 -> x1, other arithmetic: none -> 0.72 us  [on_device(): pair = jnp.concatenate([diffusivity.T, obs_weight.T], axis=0)]
where the time goes in v3:
time: 35.3 us; the launch traced here: 35 us
  Pallas kernels  32.6 us (92%)
  local copies, waits for them, and re-layouts  1.67 us (5%)
  other arithmetic  0.72 us (2%)
    pallas_call x1, Pallas kernels, on_device(): pl.pallas_call(functools.partial(kernel, lons, lats), out_shape=jax.Shape...  32.6 us
    unnamed x3, local copies, waits for them, and re-layouts  1.67 us
    concatenate x1, other arithmetic, on_device(): pair = jnp.concatenate([diffusivity.T, obs_weight.T], axis=0)  0.72 us

profile of v3, /device:TPU:1, one launch (start us, length us, event | category | flops | bytes accessed | tf_op | source)
XLA Modules:
  0.0 35.0 jit_solution(1394833642286139672)
XLA Ops:
  0.0 0.7 %pad_maximum_fusion.pair = f32[32,32]{1,0:T(8,128)S(1)} fusion(f32[16,32]{1,0:T(8,128)} %bitcast.4, f32[16,32]{1,0:T(8,128)} %bitcast.5), kind=kLoop, calls=%fused_computation | loop fusion | flops 1024 | bytes 8192 | tf_op jit(solution)/shard_map/concatenate | solution.py:362
  0.7 0.0 copy-start
  0.7 0.7 %copy-done = s32[32,16]{0,1:T(8,128)S(1)} copy-done((s32[32,16]{0,1:T(8,128)S(1)}, s32[32,16]{0,1:T(8,128)}, u32[]{:S(2)}) %copy-start) | copy-done | bytes 2072
  1.4 32.6 %shard_map.73 = f32[4,32,16,128]{3,2,1,0:T(8,128)S(1)} custom-call(f32[4,32,16,128]{3,2,1,0:T(8,128)} %ctl.1, f32[4,32,16,128]{3,2,1,0:T(8,128)} %obs.1, f32[4,32,16,128]{3,2,1,0:T(8,128)} %dev.1, f32[32,32]{1,0:T(8,128)S(1)} %pad_maximum_fusion.pair, s32[16,32]{1,0:T(8,128)S(1)} %bitcast.3, f32[16,4,128,128]{3,2,1,0:T(8,128)} %cor.1), custom_call_target="tpu_custom_call" | custom-call | flops 1000000000 | bytes 8388608 | tf_op jit(solution)/shard_map/pallas_call | solution.py:364
  34.1 1.0 %copy.9 = f32[4,32,16,128]{3,2,1,0:T(8,128)} copy(f32[4,32,16,128]{3,2,1,0:T(8,128)S(1)} %shard_map.73) | data formatting | bytes 2097152
Async XLA Ops:
  0.7 0.7 %copy-start = (s32[32,16]{0,1:T(8,128)S(1)}, s32[32,16]{0,1:T(8,128)}, u32[]{:S(2)}) copy-start(s32[32,16]{0,1:T(8,128)} %param.12) | copy-start | bytes 6148

commit v4 on v3

--- a/solution.py
+++ b/solution.py
@@ -52,8 +52,8 @@
 
 def kernel(
     lons, lats,
-    ctl, obs, dev, pair, reg, cor, out,
-    u1, u2, ct, ob, dv, corr, split, c0, cx, cw, cy, wb, regions, dt, dr,
+    ctl, obs, dev, cells, cor, out,
+    u1, u2, ct, ob, dv, corr, split, c0, cx, cw, cy, wb, region_rows, regions, dt, dr,
     side_out, corner_out, side_in, corner_in,
     send_sem, recv_sem, dsend_sem, drecv_sem, small_sem, load_sem,
 ):
@@ -79,7 +79,7 @@
         guarded(side, lambda side=side: pl.semaphore_signal(
             barrier, inc=1, device_id=neighbour(side), device_id_type=MESH))
 
-    region_copy = pltpu.make_async_copy(reg, regions, small_sem.at[0])
+    region_copy = pltpu.make_async_copy(region_rows, regions, small_sem.at[0])
 
     def own(ref, v):
         return ref.at[v, pl.ds(top, height), pl.ds(left, width)]
@@ -97,6 +97,7 @@
     for kind in range(4):
         for v in range(variables):
             load(kind, v).start()
+    region_rows[...] = jnp.clip(cells[2 * width:3 * width].astype(jnp.int32), 0, corr.shape[1] - 1)
     region_copy.start()
 
     def message(phase, v, side):
@@ -152,8 +153,8 @@
             guarded(side, lambda side=side: message(phase, v, side).start())
 
     dt[...] = jnp.zeros_like(dt)
-    dt[:, 0:height] = pair[0:width]
-    weight_t = pair[width:2 * width]
+    dt[:, 0:height] = cells[0:width]
+    weight_t = cells[width:2 * width]
 
     load(0, 0).wait()
     pack(u1, 0, 0)
@@ -359,12 +360,12 @@
     variables, height, width, levels = control.shape
     regions = correlation.shape[0]
     padded = (variables, height + 2 * HALO, width + 16, levels)
-    pair = jnp.concatenate([diffusivity.T, obs_weight.T], axis=0)
+    cells = sum(jnp.pad(x.T, ((n * width, (2 - n) * width), (0, 0))).astype(F32) for n, x in enumerate((diffusivity, obs_weight, region_map)))
     in_hbm = pl.BlockSpec(memory_space=pltpu.HBM)
     return pl.pallas_call(
         functools.partial(kernel, lons, lats),
         out_shape=jax.ShapeDtypeStruct(control.shape, F32),
-        in_specs=[in_hbm] * 3 + [pl.BlockSpec(memory_space=pltpu.VMEM)] + [in_hbm] * 2,
+        in_specs=[in_hbm] * 3 + [pl.BlockSpec(memory_space=pltpu.VMEM)] + [in_hbm],
         out_specs=pl.BlockSpec(memory_space=pltpu.VMEM),
         scratch_shapes=[
             pltpu.VMEM(padded, F32),
@@ -379,6 +380,7 @@
             pltpu.VMEM((height + 2 * HALO, width + 2 * HALO, levels), F32),
             pltpu.VMEM((height + 2 * HALO, width + 2 * HALO, levels), F32),
             pltpu.VMEM((height, width, levels), F32),
+            pltpu.VMEM((width, height), jnp.int32),
             pltpu.SMEM((width, height), jnp.int32),
             pltpu.VMEM((width, 128), F32),
             pltpu.VMEM((8, width, 128), F32),
@@ -396,7 +398,7 @@
         compiler_params=pltpu.CompilerParams(
             collective_id=0, has_side_effects=True, vmem_limit_bytes=52 * 2**20),
         cost_estimate=pl.CostEstimate(flops=10**9, bytes_accessed=8 * 2**20, transcendentals=0),
-    )(control, observed, deviation, pair, region_map.T, correlation)
+    )(control, observed, deviation, cells, correlation)
 
 
 def solution(mesh):

time: 35.3 us -> 34.5 us (0.977)
  local copies, waits for them, and re-layouts: 1.67 us -> 0.97 us
    add x0 -> x1, other arithmetic: none -> 0.73 us  [on_device(): sum((jnp.pad(x.T, ((n * width, (2 - n) * width), (0, 0))).astype(F32) for...]
    concatenate x1 -> x0, other arithmetic: 0.72 us -> none  [on_device(): pair = jnp.concatenate([diffusivity.T, obs_weight.T], axis=0)]
    unnamed x3 -> x1, local copies, waits for them, and re-layouts: 1.67 us -> 0.97 us
where the time goes in v4:
time: 34.5 us; the launch traced here: 34.4 us
  Pallas kernels  32.6 us (94%)
  local copies, waits for them, and re-layouts  0.97 us (3%)
  other arithmetic  0.73 us (2%)
    pallas_call x1, Pallas kernels, on_device(): pl.pallas_call(functools.partial(kernel, lons, lats), out_shape=jax.Shape...  32.6 us
    unnamed x1, local copies, waits for them, and re-layouts  0.97 us
    add x1, other arithmetic, on_device(): sum((jnp.pad(x.T, ((n * width, (2 - n) * width), (0, 0))).astype(F32) for...  0.73 us

profile of v4, /device:TPU:1, one launch (start us, length us, event | category | flops | bytes accessed | tf_op | source)
XLA Modules:
  0.0 34.4 jit_solution(12677261886285245303)
XLA Ops:
  0.0 0.7 %convert_add_fusion.cells = f32[48,32]{1,0:T(8,128)S(1)} fusion(s32[16,32]{1,0:T(8,128)} %bitcast.3, f32[16,32]{1,0:T(8,128)} %bitcast.4, f32[16,32]{1,0:T(8,128)} %bitcast.5), kind=kLoop, calls=%fused_computation | loop fusion | flops 4608 | bytes 12288 | tf_op jit(solution)/shard_map/add | solution.py:363
  0.7 32.6 %shard_map.73 = f32[4,32,16,128]{3,2,1,0:T(8,128)S(1)} custom-call(f32[4,32,16,128]{3,2,1,0:T(8,128)} %ctl.1, f32[4,32,16,128]{3,2,1,0:T(8,128)} %obs.1, f32[4,32,16,128]{3,2,1,0:T(8,128)} %dev.1, f32[48,32]{1,0:T(8,128)S(1)} %convert_add_fusion.cells, f32[16,4,128,128]{3,2,1,0:T(8,128)} %cor.1), custom_call_target="tpu_custom_call" | custom-call | flops 1000000000 | bytes 8388608 | tf_op jit(solution)/shard_map/pallas_call | solution.py:365
  33.4 1.0 %copy.9 = f32[4,32,16,128]{3,2,1,0:T(8,128)} copy(f32[4,32,16,128]{3,2,1,0:T(8,128)S(1)} %shard_map.73) | data formatting | bytes 2097152

commit v5 on v4

--- a/solution.py
+++ b/solution.py
@@ -10,7 +10,7 @@
 PASSES = 4
 HALO = 4
 CHUNK = 16
-GROUP = 8
+GROUP = 16
 MESH = pl.DeviceIdType.MESH
 F32 = jnp.float32
 BF16 = jnp.bfloat16

time: 34.5 us -> 34.5 us (level)
  no operation moved by 1% of the time
where the time goes in v5:
time: 34.5 us; the launch traced here: 34.4 us
  Pallas kernels  32.6 us (94%)
  local copies, waits for them, and re-layouts  0.97 us (3%)
  other arithmetic  0.73 us (2%)
    pallas_call x1, Pallas kernels, on_device(): pl.pallas_call(functools.partial(kernel, lons, lats), out_shape=jax.Shape...  32.6 us
    unnamed x1, local copies, waits for them, and re-layouts  0.97 us
    add x1, other arithmetic, on_device(): sum((jnp.pad(x.T, ((n * width, (2 - n) * width), (0, 0))).astype(F32) for...  0.73 us

profile of v5, /device:TPU:1, one launch (start us, length us, event | category | flops | bytes accessed | tf_op | source)
XLA Modules:
  0.0 34.4 jit_solution(12677261886285245303)
XLA Ops:
  0.0 0.7 %convert_add_fusion.cells = f32[48,32]{1,0:T(8,128)S(1)} fusion(s32[16,32]{1,0:T(8,128)} %bitcast.3, f32[16,32]{1,0:T(8,128)} %bitcast.4, f32[16,32]{1,0:T(8,128)} %bitcast.5), kind=kLoop, calls=%fused_computation | loop fusion | flops 4608 | bytes 12288 | tf_op jit(solution)/shard_map/add | solution.py:363
  0.7 32.6 %shard_map.73 = f32[4,32,16,128]{3,2,1,0:T(8,128)S(1)} custom-call(f32[4,32,16,128]{3,2,1,0:T(8,128)} %ctl.1, f32[4,32,16,128]{3,2,1,0:T(8,128)} %obs.1, f32[4,32,16,128]{3,2,1,0:T(8,128)} %dev.1, f32[48,32]{1,0:T(8,128)S(1)} %convert_add_fusion.cells, f32[16,4,128,128]{3,2,1,0:T(8,128)} %cor.1), custom_call_target="tpu_custom_call" | custom-call | flops 1000000000 | bytes 8388608 | tf_op jit(solution)/shard_map/pallas_call | solution.py:365
  33.4 1.0 %copy.9 = f32[4,32,16,128]{3,2,1,0:T(8,128)} copy(f32[4,32,16,128]{3,2,1,0:T(8,128)S(1)} %shard_map.73) | data formatting | bytes 2097152

commit v6 on v4

--- a/solution.py
+++ b/solution.py
@@ -334,6 +334,8 @@
     @pl.loop(0, variables)
     def _(v):
         load(4, v).wait()
+        for side in range(8):
+            guarded(side, lambda side=side: message(0, v, side).wait_send())
         arrive(u2, 1, v)
         for side in (2, 3):
             guarded(side, lambda side=side: message(1, v, side).wait_send())
@@ -347,10 +349,8 @@
 
     @pl.loop(0, variables)
     def _(v):
-        for phase in range(2):
-            for side in range(8):
-                if phase == 0 or side not in (2, 3):
-                    guarded(side, lambda: message(phase, v, side).wait_send())
+        for side in (0, 1, 4, 5, 6, 7):
+            guarded(side, lambda side=side: message(1, v, side).wait_send())
 
     for side in range(8):
         guarded(side, lambda side=side: coefficients(side).wait_send())

time: 34.5 us -> 34.5 us (level)
  no operation moved by 1% of the time
where the time goes in v6:
time: 34.5 us; the launch traced here: 34.3 us
  Pallas kernels  32.6 us (94%)
  local copies, waits for them, and re-layouts  0.97 us (3%)
  other arithmetic  0.73 us (2%)
    pallas_call x1, Pallas kernels, on_device(): pl.pallas_call(functools.partial(kernel, lons, lats), out_shape=jax.Shape...  32.6 us
    unnamed x1, local copies, waits for them, and re-layouts  0.97 us
    add x1, other arithmetic, on_device(): sum((jnp.pad(x.T, ((n * width, (2 - n) * width), (0, 0))).astype(F32) for...  0.73 us

profile of v6, /device:TPU:1, one launch (start us, length us, event | category | flops | bytes accessed | tf_op | source)
XLA Modules:
  0.0 34.3 jit_solution(15171255073126129505)
XLA Ops:
  0.0 0.7 %convert_add_fusion.cells = f32[48,32]{1,0:T(8,128)S(1)} fusion(s32[16,32]{1,0:T(8,128)} %bitcast.3, f32[16,32]{1,0:T(8,128)} %bitcast.4, f32[16,32]{1,0:T(8,128)} %bitcast.5), kind=kLoop, calls=%fused_computation | loop fusion | flops 4608 | bytes 12288 | tf_op jit(solution)/shard_map/add | solution.py:363
  0.7 32.6 %shard_map.73 = f32[4,32,16,128]{3,2,1,0:T(8,128)S(1)} custom-call(f32[4,32,16,128]{3,2,1,0:T(8,128)} %ctl.1, f32[4,32,16,128]{3,2,1,0:T(8,128)} %obs.1, f32[4,32,16,128]{3,2,1,0:T(8,128)} %dev.1, f32[48,32]{1,0:T(8,128)S(1)} %convert_add_fusion.cells, f32[16,4,128,128]{3,2,1,0:T(8,128)} %cor.1), custom_call_target="tpu_custom_call" | custom-call | flops 1000000000 | bytes 8388608 | tf_op jit(solution)/shard_map/pallas_call | solution.py:365
  33.3 1.0 %copy.9 = f32[4,32,16,128]{3,2,1,0:T(8,128)} copy(f32[4,32,16,128]{3,2,1,0:T(8,128)S(1)} %shard_map.73) | data formatting | bytes 2097152
